TPU v7x, 32 devices: a whole 2x2x4 slice. The times are simulated.
32 devices in a mesh: seq: 8 (over y, x, core), head: 4 (over z).
Axes of the slice: x: 2, y: 2, z: 4, core: 2. Of those that a mesh axis runs over, the one named last changes fastest.
Arguments:
- block_input: bfloat16 [32768, 768], P(('seq', 'head')), may hold values from -6 to 6
- out_cotangent: bfloat16 [32768, 768], P(('seq', 'head')), may hold values from -6 to 6
- segment_ids: int32 [32768], replicated, may hold values from 0 to 4, as said below
- in_weight: float32 [768, 3352], P(('seq', 'head')), may hold values from -0.21875 to 0.21875
- out_weight: float32 [1536, 768], P(('seq', 'head')), may hold values from -0.15625 to 0.15625
- vector_params: float32 [11336], replicated, may hold values from -13 to 2
- in_first: float32 [768, 3352], P(('seq', 'head')), may hold values from -54.3058 to 54.3058
- in_second: float32 [768, 3352], P(('seq', 'head')), may hold values from 294.912 to 2162.688
- out_first: float32 [1536, 768], P(('seq', 'head')), may hold values from -108.6116 to 108.6116
- out_second: float32 [1536, 768], P(('seq', 'head')), may hold values from 1212.416 to 8519.68
- vector_first: float32 [11336], replicated, may hold values from -54.3058 to 54.3058
- vector_second: float32 [11336], replicated, may hold values from 294.912 to 2162.688
Outputs:
- block_output: bfloat16 [32768, 768], P(('seq', 'head'))
- input_grad: bfloat16 [32768, 768], P(('seq', 'head'))
- in_first_new: float32 [768, 3352], P(('seq', 'head'))
- in_second_new: float32 [768, 3352], P(('seq', 'head'))
- in_weight_new: float32 [768, 3352], P(('seq', 'head'))
- out_first_new: float32 [1536, 768], P(('seq', 'head'))
- out_second_new: float32 [1536, 768], P(('seq', 'head'))
- out_weight_new: float32 [1536, 768], P(('seq', 'head'))
- vector_first_new: float32 [11336], replicated
- vector_second_new: float32 [11336], replicated
- vector_new: float32 [11336], replicated
Inputs may be any that keep to these rules, and one draw needn't show every extreme that they name: `segment_ids`: never falls along the tokens; starts at 0 and ends at 4; one document begins within the first 4096 tokens and ends within the last 4096.
All inputs are finite; a program needn't handle non-finite values.
Results may differ from a plain program's by a relative error of at most 0.011.
Values may be sent and summed in bfloat16 or wider, within the bound.
No kernel may reach another device: no remote copies, remote signals or barrier semaphores. Data moves between devices by JAX's collectives and lax.ppermute only.
A program may use at most 256 MiB of HBM per device.

v0:
```python
import functools

import jax
import jax.numpy as jnp
from jax import lax
from jax.experimental import pallas as pl
from jax.experimental.pallas import tpu as pltpu
from jax.sharding import PartitionSpec as P

WIDTH = 768
INNER = 1536
HEADS = 24
HEAD_SIZE = 64
STATE = 128
CONV_WIDTH = 4
STRETCH = 256
STEP = 10
CONV_CHANNELS = 1792
LANES = 128
PAIRS = HEADS // 2
MIXED = CONV_CHANNELS + LANES
HALO = 16
CHUNK = 32
PART = 64
LOG2E = 1.4426950408889634
HALF = STRETCH // 2
TILE = 384

EPS = 1e-05
BETA_ONE = 0.9
BETA_TWO = 0.95
ADAM_EPS = 1e-08
WEIGHT_DECAY = 0.1
RATE_MATRIX = 0.05
RATE_VECTOR = 0.3
HIGHEST = lax.Precision.HIGHEST
f32 = jnp.float32
bf16 = jnp.bfloat16
EVERY = ("seq", "head")
ROOM = 56 * 1024 * 1024


def passed_along(value, axis, steps):
    count = lax.axis_size(axis)
    leading, last = (max(0, -steps), min(count, count - steps))
    return lax.ppermute(value, axis, [(source, source + steps) for source in range(leading, last)])


def fetched(value, axis, bit):
    return lax.ppermute(value, axis, [(k, k ^ bit) for k in range(lax.axis_size(axis))])


def laid(pieces):
    rows, width = pieces[0][1].shape
    whole_array = jnp.zeros((rows * len(pieces), width), pieces[0][1].dtype)
    for place, piece in pieces:
        whole_array = lax.dynamic_update_slice(whole_array, piece, (place * rows, 0))
    return whole_array


def split_vector(vector):
    cursor = 0
    pieces = []
    for length in (WIDTH, INNER, CONV_WIDTH * CONV_CHANNELS, CONV_CHANNELS, HEADS, HEADS, HEADS):
        pieces.append(vector[cursor : cursor + length])
        cursor = cursor + length
    norm_gain, gated_gain, conv_flat, conv_bias, step_bias, log_rate, skip_gain = pieces
    return (
        norm_gain,
        gated_gain,
        conv_flat.reshape(CONV_WIDTH, CONV_CHANNELS),
        conv_bias,
        step_bias,
        log_rate,
        skip_gain,
    )


def adamw(weight, first, second, grad, rate, decay):
    first_new = BETA_ONE * first + (1.0 - BETA_ONE) * grad
    second_new = BETA_TWO * second + (1.0 - BETA_TWO) * grad * grad
    corrected_first = first_new / (1.0 - BETA_ONE**STEP)
    corrected_second = second_new / (1.0 - BETA_TWO**STEP)
    weight_new = weight - rate * (
        corrected_first / (jnp.sqrt(corrected_second) + ADAM_EPS) + decay * weight
    )
    return (first_new, second_new, weight_new)


def mm(left, right, dims=((1,), (0,)), precision=None):
    return lax.dot_general(left, right, (dims, ((), ())), preferred_element_type=f32, precision=precision)


NT = ((1,), (1,))
TN = ((0,), (0,))


def spec(block, index):
    return pl.BlockSpec(block, index)


def whole(*shape):
    return pl.BlockSpec(shape, lambda *ids: (0,) * len(shape))


def call(body, grid, ins, outs, out_shapes, scratch, micros):
    return pl.pallas_call(
        body,
        grid=grid,
        in_specs=ins,
        out_specs=outs,
        out_shape=[jax.ShapeDtypeStruct(shape, kind) for shape, kind in out_shapes],
        scratch_shapes=scratch,
        compiler_params=pltpu.CompilerParams(vmem_limit_bytes=ROOM),
        cost_estimate=pl.CostEstimate(flops=0, bytes_accessed=int(micros * 3.4e6), transcendentals=0),
    )


def in_two(value):
    top = value.astype(bf16)
    return top, (value - top.astype(f32)).astype(bf16)


def spread_heads(per_head, spreader):
    return mm(jnp.concatenate(in_two(per_head), axis=1), spreader)


def eights(value):
    return jnp.sum(value.reshape(value.shape[0] // 8, 8, value.shape[1]), axis=0)


def tiles(width):
    return [slice(j * LANES, (j + 1) * LANES) for j in range(width // LANES)]


def chunks(count, size, body):
    def step(i, _):
        body(pl.ds(pl.multiple_of(i * size, size), size))
        return 0

    lax.fori_loop(0, count // size, step, 0, unroll=2)


def sigmoid(v):
    return 0.5 * jnp.tanh(0.5 * v) + 0.5


def softplus(v):
    small = jnp.exp(-jnp.abs(v))
    series = small * (1.0 - small * (0.5 - small * (1.0 / 3.0 - small * 0.25)))
    return jnp.maximum(v, 0.0) + jnp.where(small < 0.01, series, jnp.log(1.0 + small))


def spread_masks(masks, same):
    @pl.when(pl.program_id(0) == 0)
    def _():
        for k in range(1, CONV_WIDTH):
            same[k - 1] = jnp.broadcast_to(masks[:, k - 1 : k], same.shape[1:])


def hold(mixed, held):
    count = mixed.shape[0] - HALO
    for j, cols in enumerate(tiles(TILE)):
        held[j, :HALO, :] = mixed[count:, cols].astype(f32)
        held[j, HALO:, :] = mixed[:count, cols].astype(f32)


def conv_part(held, same, taps, rows, cols):
    taken = [held[cols.start // LANES, pl.ds(HALO + rows - k, PART), :] for k in range(CONV_WIDTH)]
    total = taps[CONV_WIDTH : CONV_WIDTH + 1, cols] + taps[3:4, cols] * taken[0]
    for k in range(1, CONV_WIDTH):
        total = total + taps[3 - k : 4 - k, cols] * (taken[k] * same[k - 1, rows : rows + PART, :])
    return total, taken


def each_tile(convolve, other):
    for cols in tiles(TILE)[:-1]:
        convolve(cols)
    ending = pl.program_id(0) == pl.num_programs(0) - 1
    cols = tiles(TILE)[-1]
    pl.when(jnp.logical_not(ending))(lambda: convolve(cols))
    pl.when(ending)(lambda: other(cols))


def conv_forward(bits, where, normed, masks, taps, *others):
    pieces, (out, mixed, weight_out, held, same, weight) = others[: len(bits)], others[len(bits) :]
    count = out.shape[0]
    spread_masks(masks, same)
    size = pieces[0].shape[0]
    for bit, piece in zip(bits, pieces):
        start = pl.multiple_of((where[0] ^ bit) * size, 8)
        weight[pl.ds(start, size), :] = piece[...].astype(f32)
    weight_out[...] = weight[...].astype(bf16)
    low = mm(normed[...], weight_out[...]).astype(bf16)
    mixed[...] = low
    hold(low, held)

    def convolve(cols):
        for rows in range(0, count, PART):
            total, _ = conv_part(held, same, taps, rows, cols)
            out[rows : rows + PART, cols] = (total * sigmoid(total)).astype(bf16)

    def other(cols):
        out[:, cols] = mixed[:count, cols]

    each_tile(convolve, other)


def local_states(
    values, both, raw, masks, bias, rate, spreader,
    scaled, cumul_out, delta_out, cumul_rows, start, factors, device_state, device_decay,
    state, reach, weighted, steps, ends,
):
    c = pl.program_id(0)

    @pl.when(c == 0)
    def _():
        state[...] = jnp.zeros_like(state)
        reach[...] = jnp.ones_like(reach)

    delta = softplus(raw[...].astype(f32) + bias[...])
    row = lax.broadcasted_iota(jnp.int32, (STRETCH, STRETCH), 0)
    col = lax.broadcasted_iota(jnp.int32, (STRETCH, STRETCH), 1)
    cumul = mm((row >= col).astype(f32), delta * rate[...], precision=HIGHEST)
    last = cumul[STRETCH - 1 : STRETCH, :]
    carry = jnp.exp(last) * masks[STRETCH - 1 : STRETCH, 4:5]
    cumul_out[...] = cumul
    delta_out[...] = delta
    cumul_rows[0] = cumul.T[: cumul_rows.shape[1], :] * LOG2E
    steps[...] = spread_heads(delta, spreader[...])
    ends[...] = spread_heads(jnp.exp(last - cumul) * masks[:, 3:4] * delta, spreader[...])
    for cols in tiles(INNER):
        v = values[:, cols].astype(f32)
        scaled[:, cols] = (v * steps[:, cols]).astype(bf16)
        weighted[:, cols] = (v * ends[:, cols]).astype(bf16)
    start[0] = state[...].astype(bf16)
    line = lax.broadcasted_iota(jnp.int32, (8, LANES), 0)
    wide = spread_heads(jnp.where(line == 0, carry, reach[...]), spreader[...])
    factors[0] = wide
    state[...] = state[...] * wide[0:1, :] + mm(both[:, :STATE], weighted[...], TN)
    reach[...] = reach[...] * carry

    @pl.when(c == pl.num_programs(0) - 1)
    def _():
        for j, cols in enumerate(tiles(INNER)):
            device_state[j] = state[:, cols].astype(bf16)
        device_decay[...] = reach[...]


def spread_columns(cumul, columns):
    for h in range(HEADS):
        columns[h] = jnp.broadcast_to(cumul[:, h : h + 1] * LOG2E, (STRETCH, LANES))


def diagonal(scaled, both, cumul, cumul_rows, masks, segments, out, columns, scores):
    spread_columns(cumul, columns)
    row = lax.broadcasted_iota(jnp.int32, (STRETCH, STRETCH), 0)
    col = lax.broadcasted_iota(jnp.int32, (STRETCH, STRETCH), 1)
    inside = (row >= col) & (masks[:, 5:6] == segments[0])
    scores[...] = jnp.where(inside, mm(both[:, STATE:], both[:, :STATE], NT), 0.0)
    low = lax.broadcasted_iota(jnp.int32, (HALF, LANES), 1) < HEAD_SIZE

    def pair(j, _):
        cols = pl.ds(pl.multiple_of(j * LANES, LANES), LANES)
        v = scaled[:, cols]
        tops, bottoms = [], []
        for q in range(2):
            h = 2 * j + q
            line = cumul_rows[0, pl.ds(h, 1), :]
            upper = columns[h, :HALF, :]
            lower = columns[h, HALF:, :]
            top = jnp.exp2(jnp.minimum(upper - line[:, :HALF], 0.0)) * scores[:HALF, :HALF]
            left = jnp.exp2(jnp.minimum(lower - line[:, :HALF], 0.0)) * scores[HALF:, :HALF]
            right = jnp.exp2(jnp.minimum(lower - line[:, HALF:], 0.0)) * scores[HALF:, HALF:]
            tops.append(mm(top.astype(bf16), v[:HALF]))
            bottoms.append(mm(jnp.concatenate([left.astype(bf16), right.astype(bf16)], axis=1), v))
        out[:HALF, cols] = jnp.where(low, *tops)
        out[HALF:, cols] = jnp.where(low, *bottoms)
        return 0

    lax.fori_loop(0, PAIRS, pair, 0, unroll=2)


def diagonal_back(
    scaled, both, cumul, cumul_rows, masks, segments, out_grad, sums, both_grad, columns, scores, total
):
    spread_columns(cumul, columns)
    row = lax.broadcasted_iota(jnp.int32, (STRETCH, STRETCH), 0)
    col = lax.broadcasted_iota(jnp.int32, (STRETCH, STRETCH), 1)
    inside = (row <= col) & (masks[:, 5:6] == segments[0])
    scores[...] = jnp.where(inside, mm(both[:, :STATE], both[:, STATE:], NT), 0.0)
    total[...] = jnp.zeros_like(total)
    low = lax.broadcasted_iota(jnp.int32, (HALF, LANES), 1) < HEAD_SIZE
    first = lax.broadcasted_iota(jnp.int32, (STRETCH, LANES), 1) < HEAD_SIZE

    def pair(j, _):
        cols = pl.ds(pl.multiple_of(j * LANES, LANES), LANES)
        v = scaled[:, cols]
        g = out_grad[:, cols]
        tops, bottoms = [], []
        for q in range(2):
            h = 2 * j + q
            line = cumul_rows[0, pl.ds(h, 1), :]
            upper = columns[h, :HALF, :]
            lower = columns[h, HALF:, :]
            own = jnp.where(first == (q == 0), g.astype(f32), 0.0).astype(bf16)
            left = jnp.exp2(jnp.minimum(line[:, :HALF] - upper, 0.0))
            right = jnp.exp2(jnp.minimum(line[:, HALF:] - upper, 0.0))
            corner = jnp.exp2(jnp.minimum(line[:, HALF:] - lower, 0.0))
            tops.append(
                mm(
                    jnp.concatenate(
                        [(left * scores[:HALF, :HALF]).astype(bf16), (right * scores[:HALF, HALF:]).astype(bf16)],
                        axis=1,
                    ),
                    g,
                )
            )
            bottoms.append(mm((corner * scores[HALF:, HALF:]).astype(bf16), g[HALF:]))
            top_grad = mm(v[:HALF], own, NT)
            total[:HALF, :HALF] += left * top_grad[:, :HALF]
            total[:HALF, HALF:] += right * top_grad[:, HALF:]
            total[HALF:, HALF:] += corner * mm(v[HALF:], own[HALF:], NT)
        sums[:HALF, cols] = jnp.where(low, *tops)
        sums[HALF:, cols] = jnp.where(low, *bottoms)
        return 0

    lax.fori_loop(0, PAIRS, pair, 0, unroll=2)
    scores_grad = jnp.where(inside, total[...], 0.0).astype(bf16)
    both_grad[:, :STATE] = mm(scores_grad, both[:, STATE:])
    both_grad[:, STATE:] = mm(scores_grad, both[:, :STATE], TN)


def prefix(parts, decays, second, out, reverse):
    count = parts.shape[0]
    rows = out.shape[1]

    def step(i, state):
        k = count - 1 - i if reverse else i
        out[pl.ds(k, 1)] = state.astype(bf16)[None]
        two = decays[pl.ds(k, 1)][0]
        decay = jnp.where(second[...] > 0.0, two[1:2, :], two[0:1, :])
        return decay * state + parts[pl.ds(k, 1), :rows, :][0].astype(f32)

    lax.fori_loop(0, count, step, jnp.zeros((rows, LANES), f32))


def head_sums(products, heads):
    return sum(mm(product[...], heads[...]) for product in products)


def entered(start, factors, prior, j, cols):
    return start[0, :, cols].astype(f32) + factors[0, 1:2, cols] * prior[j].astype(f32)


def middle(
    diag, values, both, cumul, masks, start, factors, prior, gate, normed_grad, gain, skip, heads,
    spreader,
    gated_low, gate_grad, mixed_grad, row_sums, reads_grad, after_local, sums, start_grad,
    after_decay, full, entry, enter, gated_all, sig_all, mixed_all, entry_low, high, low, state_grad, tail_decay,
):
    i = pl.program_id(0)

    @pl.when(i == 0)
    def _():
        state_grad[...] = jnp.zeros_like(state_grad)
        tail_decay[...] = jnp.ones_like(tail_decay)
        sums[...] = jnp.zeros_like(sums)

    reads = both[:, STATE:]
    for j, cols in enumerate(tiles(INNER)):
        full[:, cols] = entered(start, factors, prior, j, cols).astype(bf16)
    entry[...] = mm(reads, full[...])
    enter[...] = spread_heads(jnp.exp(cumul[...]) * masks[:, 4:5], spreader[...])

    def rows_step(rows):
        square = jnp.zeros((CHUNK, LANES), f32)
        cross = jnp.zeros((CHUNK, LANES), f32)
        for cols in tiles(INNER):
            mixed_sum = diag[rows, cols] + entry[rows, cols] * enter[rows, cols]
            mixed = (mixed_sum + skip[:, cols] * values[rows, cols].astype(f32)).astype(bf16)
            z = gate[rows, cols]
            sig = sigmoid(z)
            gated = mixed.astype(f32) * (z * sig)
            square = square + gated * gated
            cross = cross + (normed_grad[rows, cols] * gain[:, cols]) * gated
            entry[rows, cols] = mixed_sum
            gated_all[rows, cols] = gated
            sig_all[rows, cols] = sig
            mixed_all[rows, cols] = mixed
        scale = lax.rsqrt(jnp.sum(square, axis=1, keepdims=True) * (1.0 / INNER) + EPS)
        pull = jnp.sum(cross, axis=1, keepdims=True) * (1.0 / INNER) * (scale * scale * scale)
        scale = jnp.broadcast_to(scale, (CHUNK, LANES))
        pull = jnp.broadcast_to(pull, (CHUNK, LANES))
        for cols in tiles(INNER):
            gated = gated_all[rows, cols]
            sig = sig_all[rows, cols]
            back = normed_grad[rows, cols]
            unit = gated * scale
            gated_low[rows, cols] = (unit * gain[:, cols]).astype(bf16)
            gated_grad = scale * (back * gain[:, cols]) - gated * pull
            act = gate[rows, cols] * sig
            slope = sig + act * (1.0 - sig)
            gate_grad[rows, cols] = (gated_grad * mixed_all[rows, cols].astype(f32) * slope).astype(bf16)
            low_grad = (gated_grad * act).astype(bf16)
            mixed_grad[rows, cols] = low_grad
            grad = low_grad.astype(f32)
            entry_low[rows, cols] = (grad * enter[rows, cols]).astype(bf16)
            high[rows, cols], low[rows, cols] = in_two(grad * entry[rows, cols])
            sums[0:8, cols] += eights(back * unit)
            sums[8:16, cols] += eights(grad * values[rows, cols].astype(f32))

    chunks(STRETCH, CHUNK, rows_step)
    row_sums[...] = head_sums((high, low), heads)
    reads_grad[...] = mm(entry_low[...], full[...], NT)
    after_local[0] = state_grad[...].astype(bf16)
    after_decay[0] = tail_decay[...]
    state_grad[...] = state_grad[...] * factors[0, 0:1, :] + mm(reads, entry_low[...], TN)
    tail_decay[...] = tail_decay[...] * factors[0, 0:1, :]

    @pl.when(i == pl.num_programs(0) - 1)
    def _():
        for j, cols in enumerate(tiles(INNER)):
            start_grad[j] = state_grad[:, cols].astype(bf16)


def late(
    values, both, cumul, delta, raw, masks, bias, rate, factors, start, prior, after_local, after_decay, after,
    diag_sums, scaled, out_grad, row_sums, reads_grad, both_grad, skip, heads, spreader,
    conv_grad, sums,
    after_low, spread_grad, factor, wide, weighted, joint, outer_low, high, low,
):
    @pl.when(pl.program_id(0) == 0)
    def _():
        sums[...] = jnp.zeros_like(sums)

    carry_rows = []
    for j, cols in enumerate(tiles(INNER)):
        here = after_local[0, :, cols].astype(f32) + after_decay[0, 0:1, cols] * after[j].astype(f32)
        after_low[:, cols] = here.astype(bf16)
        carry_rows.append(eights(here * entered(start, factors, prior, j, cols)) * factors[0, 0:1, cols])
    carry_grad = sum(mm(part, heads[...]) for part in in_two(jnp.concatenate(carry_rows, axis=1)))
    spread_grad[...] = mm(both[:, :STATE], after_low[...])
    step = delta[...]
    total = cumul[...]
    end_factor = jnp.exp(total[STRETCH - 1 : STRETCH, :] - total) * masks[:, 3:4]
    factor[...] = spread_heads(end_factor, spreader[...])
    wide[...] = spread_heads(step, spreader[...])

    def rows_step(rows):
        for cols in tiles(INNER):
            v = values[rows, cols].astype(f32)
            ends = factor[rows, cols]
            step_wide = wide[rows, cols]
            inner = diag_sums[rows, cols]
            outer = spread_grad[rows, cols] * ends
            both_sums = inner + outer
            conv_grad[rows, cols] = (
                step_wide * both_sums + skip[:, cols] * out_grad[rows, cols].astype(f32)
            ).astype(bf16)
            weighted[rows, cols] = (v * (ends * step_wide)).astype(bf16)
            joint[rows, cols] = (v * both_sums).astype(bf16)
            outer_low[rows, cols] = (v * outer).astype(bf16)
            high[rows, cols], low[rows, cols] = in_two(scaled[rows, cols].astype(f32) * inner)

    chunks(STRETCH, CHUNK, rows_step)
    conv_grad[:, INNER : INNER + STATE] = (
        both_grad[:, :STATE] + mm(weighted[...], after_low[...], NT)
    ).astype(bf16)
    conv_grad[:, INNER + STATE : CONV_CHANNELS] = (both_grad[:, STATE:] + reads_grad[...]).astype(bf16)
    end_spread = head_sums((outer_low,), heads) * step
    last_grad = jnp.sum(end_spread, axis=0, keepdims=True) + jnp.sum(carry_grad, axis=0, keepdims=True)
    cumul_grad = row_sums[...] - head_sums((high, low), heads) - end_spread
    row = lax.broadcasted_iota(jnp.int32, (STRETCH, STRETCH), 0)
    col = lax.broadcasted_iota(jnp.int32, (STRETCH, STRETCH), 1)
    decay_grad = mm((row <= col).astype(f32), cumul_grad, precision=HIGHEST) + last_grad
    step_grad = head_sums((joint,), heads) + decay_grad * rate[...]
    pre_grad = step_grad * sigmoid(raw[...].astype(f32) + bias[...])
    conv_grad[:, CONV_CHANNELS:] = pre_grad.astype(bf16)
    sums[0:1, :] += jnp.sum(decay_grad * step, axis=0, keepdims=True)
    sums[1:2, :] += jnp.sum(pre_grad, axis=0, keepdims=True)


def conv_back(mixed, grad, masks, taps, out, rim, tail, tap_grads, held, same, kept):
    rows_all = grad.shape[0]
    spread_masks(masks, same)
    hold(mixed, held)
    kept[:, :, pl.ds(rows_all, 8), :] = jnp.zeros(kept.shape[:2] + (8, LANES), f32)

    def convolve(cols):
        tile = cols.start // LANES
        found = [jnp.zeros((8, LANES), f32) for _ in range(CONV_WIDTH + 1)]
        for rows in range(0, rows_all, PART):
            total, taken = conv_part(held, same, taps, rows, cols)
            sig = sigmoid(total)
            here = grad[rows : rows + PART, cols].astype(f32) * (sig * (1.0 + total * (1.0 - sig)))
            found[CONV_WIDTH] = found[CONV_WIDTH] + eights(here)
            for k in range(CONV_WIDTH):
                masked = here if k == 0 else here * same[k - 1, rows : rows + PART, :]
                kept[k, tile, pl.ds(rows, PART), :] = masked
                found[3 - k] = found[3 - k] + eights(masked * taken[k])
        lines = [jnp.sum(line, axis=0, keepdims=True) for line in found]
        tap_grads[:, cols] = jnp.concatenate(lines + [jnp.zeros((3, LANES), f32)], axis=0)
        for rows in range(0, rows_all, PART):
            value = taps[3:4, cols] * kept[0, tile, pl.ds(rows, PART), :]
            for k in range(1, CONV_WIDTH):
                value = value + taps[3 - k : 4 - k, cols] * kept[k, tile, pl.ds(rows + k, PART), :]
            out[rows : rows + PART, cols] = value.astype(bf16)
            if rows + PART == rows_all:
                tail[:, cols] = value[PART - HALO :, :]
        lines = [jnp.zeros((5, LANES), f32)]
        for m in (3, 2, 1):
            line = jnp.zeros((1, LANES), f32)
            for k in range(m, CONV_WIDTH):
                line = line + taps[3 - k : 4 - k, cols] * kept[k, tile, k - m : k - m + 1, :]
            lines.append(line)
        rim[:, cols] = jnp.concatenate(lines, axis=0)

    def other(cols):
        out[:, cols] = grad[:, cols]
        tail[:, cols] = grad[rows_all - HALO :, cols].astype(f32)
        rim[:, cols] = jnp.zeros((8, LANES), f32)
        tap_grads[:, cols] = jnp.zeros((8, LANES), f32)

    each_tile(convolve, other)


def per_device(
    block_input,
    out_cotangent,
    segment_ids,
    in_weight,
    out_weight,
    vector_params,
    in_first,
    in_second,
    out_first,
    out_second,
    vector_first,
    vector_second,
):
    count = lax.axis_size("seq") * lax.axis_size("head")
    device_index = lax.axis_index(EVERY)
    rows = block_input.shape[0]
    stretches = rows // STRETCH
    own_rows = in_weight.shape[0]
    halo = passed_along(block_input[rows - HALO :], EVERY, 1)

    head_index, seq_index = lax.axis_index("head"), lax.axis_index("seq")
    chips = lax.axis_size("seq") // 2
    mixer_own = jnp.pad(in_weight[:, INNER:].astype(bf16), ((0, 0), (0, LANES - HEADS)))
    mixer_group = laid(
        [(head_index, mixer_own)]
        + [(head_index ^ k, fetched(mixer_own, "head", k)) for k in range(1, lax.axis_size("head"))]
    )
    mixer_group, halo, block_now, segment_now, vector_now = lax.optimization_barrier(
        (mixer_group, halo, block_input, segment_ids, vector_params)
    )
    norm_gain, gated_gain, conv_taps, conv_bias, step_bias, log_rate, skip_gain = split_vector(vector_now)

    def unit_rows(block):
        wide = block.astype(f32)
        scale = lax.rsqrt(jnp.mean(wide * wide, axis=-1, keepdims=True) + EPS)
        return wide, scale

    inputs, in_scale = unit_rows(block_now)
    normed = (inputs * in_scale * norm_gain).astype(bf16)
    halo_wide, halo_scale = unit_rows(halo)
    extended = jnp.concatenate([normed, (halo_wide * halo_scale * norm_gain).astype(bf16)], axis=0)

    padded = jnp.concatenate(
        [jnp.full((3,), -1, jnp.int32), segment_now, jnp.full((3,), -1, jnp.int32)]
    )
    window = lax.dynamic_slice_in_dim(padded, device_index * rows, rows + 6)
    own = window[3 : 3 + rows]
    blocks = own.reshape(stretches, STRETCH)
    before = window[2 : 2 + rows].reshape(stretches, STRETCH)[:, :1]
    columns = [(window[3 - k : 3 - k + rows] == own) for k in (1, 2, 3)]
    columns.append((blocks == blocks[:, -1:]).reshape(rows))
    columns.append((blocks == before).reshape(rows))
    columns.append(own)
    columns += [jnp.zeros((rows,), f32)] * 2
    masks = jnp.stack([column.astype(f32) for column in columns], axis=1)
    marks = masks.shape[1]
    segments = blocks.astype(f32).reshape(stretches, 1, STRETCH)

    taps = jnp.concatenate([conv_taps, conv_bias[None], jnp.zeros((3, CONV_CHANNELS), f32)], axis=0)
    taps = jnp.pad(taps, ((0, 0), (0, LANES)))

    def head_row(vector):
        return jnp.pad(vector, (0, LANES - HEADS)).reshape(1, LANES)

    bias_row = head_row(step_bias)
    rate_row = head_row(-jnp.exp(log_rate))
    skip_row = jnp.repeat(skip_gain, HEAD_SIZE).reshape(1, INNER)
    gain_row = gated_gain.reshape(1, INNER)
    head_of = (
        lax.broadcasted_iota(jnp.int32, (INNER, LANES), 0) // HEAD_SIZE
        == lax.broadcasted_iota(jnp.int32, (INNER, LANES), 1)
    ).astype(bf16)
    spreader = jnp.concatenate([head_of.T, head_of.T], axis=0)

    near = [(0, mixer_group)] + [(2 * k, fetched(mixer_group, "seq", 2 * k)) for k in range(1, chips)]
    near, extended, normed, masks, taps, spreader, head_of = lax.optimization_barrier(
        ([piece for _, piece in near], extended, normed, masks, taps, spreader, head_of)
    )
    bits = [2 * k for k in range(chips)] + [2 * k + 1 for k in range(chips)]
    pieces = near + [fetched(piece, "seq", 1) for piece in near]
    rest_own = jnp.concatenate([in_weight[:, :WIDTH], in_weight[:, WIDTH:INNER], out_weight], axis=0).astype(bf16)
    rest_own, pieces = lax.optimization_barrier((rest_own, pieces))
    rest = lax.all_gather(rest_own, EVERY, axis=0, tiled=True).reshape(count, -1, WIDTH)
    gate_weight = jnp.concatenate(
        [rest[:, :own_rows].reshape(WIDTH, WIDTH), rest[:, own_rows : 2 * own_rows].reshape(WIDTH, WIDTH)], axis=1
    )
    out_full = rest[:, 2 * own_rows :].reshape(INNER, WIDTH)

    convolved, mixed_low, mixer_weight = call(
        functools.partial(conv_forward, bits),
        (MIXED // TILE,),
        [
            pl.BlockSpec(memory_space=pltpu.SMEM),
            whole(rows + HALO, WIDTH),
            whole(rows, marks),
            spec((8, TILE), lambda i: (0, i)),
        ]
        + [spec((pieces[0].shape[0], TILE), lambda i: (0, i))] * len(pieces),
        [
            spec((rows, TILE), lambda i: (0, i)),
            spec((rows + HALO, TILE), lambda i: (0, i)),
            spec((WIDTH, TILE), lambda i: (0, i)),
        ],
        [((rows, MIXED), bf16), ((rows + HALO, MIXED), bf16), ((WIDTH, MIXED), bf16)],
        [
            pltpu.VMEM((TILE // LANES, rows + HALO, LANES), f32),
            pltpu.VMEM((3, rows, LANES), f32),
            pltpu.VMEM((WIDTH, TILE), f32),
        ],
        14,
    )(seq_index.reshape(1), extended, masks, taps, *pieces)

    by_block = lambda *tail: spec((STRETCH,) + tail, lambda c: (c,) + (0,) * len(tail))
    both_spec = spec((STRETCH, 2 * STATE), lambda c: (c, INNER // (2 * STATE)))
    values_spec = spec((STRETCH, INNER), lambda c: (c, 0))
    raw_spec = spec((STRETCH, LANES), lambda c: (c, CONV_CHANNELS // LANES))
    per_block = lambda *tail: spec((1,) + tail, lambda c: (c,) + (0,) * len(tail))

    scaled, cumul, delta, cumul_rows, start, factors, device_state, device_decay = call(
        local_states,
        (stretches,),
        [values_spec, both_spec, raw_spec, by_block(marks), whole(1, LANES), whole(1, LANES), whole(2 * LANES, INNER)],
        [
            by_block(INNER),
            by_block(LANES),
            by_block(LANES),
            per_block(32, STRETCH),
            per_block(STATE, INNER),
            per_block(8, INNER),
            whole(PAIRS, STATE, LANES),
            whole(8, LANES),
        ],
        [
            ((rows, INNER), bf16),
            ((rows, LANES), f32),
            ((rows, LANES), f32),
            ((stretches, 32, STRETCH), f32),
            ((stretches, STATE, INNER), bf16),
            ((stretches, 8, INNER), f32),
            ((PAIRS, STATE, LANES), bf16),
            ((8, LANES), f32),
        ],
        [
            pltpu.VMEM((STATE, INNER), f32),
            pltpu.VMEM((8, LANES), f32),
            pltpu.VMEM((STRETCH, INNER), bf16),
            pltpu.VMEM((STRETCH, INNER), f32),
            pltpu.VMEM((STRETCH, INNER), f32),
        ],
        9,
    )(convolved, convolved, convolved, masks, bias_row, rate_row, spreader)

    share = PAIRS * STATE // count
    decay_high = device_decay[0].astype(bf16)
    decay_low = (device_decay[0] - decay_high.astype(f32)).astype(bf16)
    decay_rows = jnp.broadcast_to(jnp.stack([decay_high, decay_low])[None], (count, 2, LANES))
    sent = jnp.concatenate([device_state.reshape(count, share, LANES), decay_rows], axis=1)

    def exchange(value):
        return lax.all_to_all(value, EVERY, split_axis=0, concat_axis=0, tiled=True)

    def scan_parts(parts, reverse):
        return pl.pallas_call(
            functools.partial(prefix, reverse=reverse),
            out_shape=jax.ShapeDtypeStruct((count, share, LANES), bf16),
            compiler_params=pltpu.CompilerParams(vmem_limit_bytes=ROOM),
        )(parts, pair_decays, second)

    arrived = exchange(sent)
    all_decays = arrived[:, share, :HEADS].astype(f32) + arrived[:, share + 1, :HEADS].astype(f32)
    wide_decays = jnp.repeat(all_decays, HEAD_SIZE, axis=1).reshape(count, PAIRS, LANES)
    wide_decays = jnp.pad(wide_decays, ((0, 0), (0, 1), (0, 0)))
    first_pair = device_index * share // STATE
    pair_decays = lax.dynamic_slice_in_dim(wide_decays, first_pair, 2, axis=1)
    places = device_index * share + lax.broadcasted_iota(jnp.int32, (share, LANES), 0)
    second = (places >= (first_pair + 1) * STATE).astype(f32)
    prior = exchange(scan_parts(arrived, False)).reshape(PAIRS, STATE, LANES)

    diag = call(
        diagonal,
        (stretches,),
        [
            by_block(INNER),
            both_spec,
            by_block(LANES),
            per_block(32, STRETCH),
            by_block(marks),
            per_block(1, STRETCH),
        ],
        [by_block(INNER)],
        [((rows, INNER), f32)],
        [pltpu.VMEM((HEADS, STRETCH, LANES), f32), pltpu.VMEM((STRETCH, STRETCH), f32)],
        16,
    )(scaled, convolved, cumul, cumul_rows, masks, segments)[0]
    gate = jnp.dot(normed, gate_weight, preferred_element_type=f32)
    normed_grad = mm(out_cotangent, out_full, NT)

    back = stretches - 1
    by_block_r = lambda *tail: spec((STRETCH,) + tail, lambda c: (back - c,) + (0,) * len(tail))
    per_block_r = lambda *tail: spec((1,) + tail, lambda c: (back - c,) + (0,) * len(tail))
    wide_scratch = lambda kind: pltpu.VMEM((STRETCH, INNER), kind)
    (
        gated_low,
        gate_grad,
        mixed_grad,
        row_sums,
        reads_grad,
        after_local,
        middle_sums,
        start_grad,
        after_decay,
    ) = call(
        middle,
        (stretches,),
        [
            by_block_r(INNER),
            spec((STRETCH, INNER), lambda c: (back - c, 0)),
            spec((STRETCH, 2 * STATE), lambda c: (back - c, INNER // (2 * STATE))),
            by_block_r(LANES),
            by_block_r(marks),
            per_block_r(STATE, INNER),
            per_block_r(8, INNER),
            whole(PAIRS, STATE, LANES),
            by_block_r(INNER),
            by_block_r(INNER),
            whole(1, INNER),
            whole(1, INNER),
            whole(INNER, LANES),
            whole(2 * LANES, INNER),
        ],
        [
            by_block_r(INNER),
            by_block_r(INNER),
            by_block_r(INNER),
            by_block_r(LANES),
            by_block_r(STATE),
            per_block_r(STATE, INNER),
            whole(16, INNER),
            whole(PAIRS, STATE, LANES),
            per_block_r(8, INNER),
        ],
        [
            ((rows, INNER), bf16),
            ((rows, INNER), bf16),
            ((rows, INNER), bf16),
            ((rows, LANES), f32),
            ((rows, STATE), f32),
            ((stretches, STATE, INNER), bf16),
            ((16, INNER), f32),
            ((PAIRS, STATE, LANES), bf16),
            ((stretches, 8, INNER), f32),
        ],
        [
            pltpu.VMEM((STATE, INNER), bf16),
            wide_scratch(f32),
            wide_scratch(f32),
            wide_scratch(f32),
            wide_scratch(f32),
            wide_scratch(bf16),
            wide_scratch(bf16),
            wide_scratch(bf16),
            wide_scratch(bf16),
            pltpu.VMEM((STATE, INNER), f32),
            pltpu.VMEM((8, INNER), f32),
        ],
        24,
    )(
        diag, convolved, convolved, cumul, masks, start, factors, prior, gate, normed_grad,
        gain_row, skip_row, head_of, spreader,
    )

    sent_back = exchange(start_grad.reshape(count, share, LANES))
    diag_sums, both_grad = call(
        diagonal_back,
        (stretches,),
        [
            by_block(INNER),
            both_spec,
            by_block(LANES),
            per_block(32, STRETCH),
            by_block(marks),
            per_block(1, STRETCH),
            by_block(INNER),
        ],
        [by_block(INNER), by_block(2 * STATE)],
        [((rows, INNER), f32), ((rows, 2 * STATE), f32)],
        [
            pltpu.VMEM((HEADS, STRETCH, LANES), f32),
            pltpu.VMEM((STRETCH, STRETCH), f32),
            pltpu.VMEM((STRETCH, STRETCH), f32),
        ],
        20,
    )(scaled, convolved, cumul, cumul_rows, masks, segments, mixed_grad)
    sent_back, diag_sums, both_grad = lax.optimization_barrier((sent_back, diag_sums, both_grad))
    scanned = scan_parts(sent_back, True)
    gated_low, gate_grad, scanned = lax.optimization_barrier((gated_low, gate_grad, scanned))
    after = exchange(scanned)
    block_output = (inputs + mm(gated_low, out_full)).astype(bf16)

    gate_term = mm(normed, gate_grad, TN).astype(bf16)
    out_term = mm(gated_low, out_cotangent, TN).astype(bf16)
    rest_term = jnp.concatenate(
        [
            gate_term[:, :WIDTH].reshape(count, -1, WIDTH),
            gate_term[:, WIDTH:].reshape(count, -1, WIDTH),
            out_term.reshape(count, -1, WIDTH),
        ],
        axis=1,
    ).reshape(-1, WIDTH)
    rest_term, block_output, after = lax.optimization_barrier((rest_term, block_output, after))
    after = after.reshape(PAIRS, STATE, LANES)
    rest_line = lax.psum_scatter(rest_term, "seq", scatter_dimension=0, tiled=True)

    conv_out_grad, late_sums = call(
        late,
        (stretches,),
        [
            values_spec,
            both_spec,
            by_block(LANES),
            by_block(LANES),
            raw_spec,
            by_block(marks),
            whole(1, LANES),
            whole(1, LANES),
            per_block(8, INNER),
            per_block(STATE, INNER),
            whole(PAIRS, STATE, LANES),
            per_block(STATE, INNER),
            per_block(8, INNER),
            whole(PAIRS, STATE, LANES),
            by_block(INNER),
            by_block(INNER),
            by_block(INNER),
            by_block(LANES),
            by_block(STATE),
            by_block(2 * STATE),
            whole(1, INNER),
            whole(INNER, LANES),
            whole(2 * LANES, INNER),
        ],
        [by_block(MIXED), whole(8, LANES)],
        [((rows, MIXED), bf16), ((8, LANES), f32)],
        [
            pltpu.VMEM((STATE, INNER), bf16),
            wide_scratch(f32),
            wide_scratch(f32),
            wide_scratch(f32),
        ]
        + [wide_scratch(bf16)] * 5,
        18,
    )(
        convolved, convolved, cumul, delta, convolved, masks, bias_row, rate_row, factors, start, prior, after_local, after_decay,
        after, diag_sums, scaled, mixed_grad, row_sums, reads_grad, both_grad, skip_row, head_of, spreader,
    )

    mixed_in_grad, rim, tail, tap_grads = call(
        conv_back,
        (MIXED // TILE,),
        [
            spec((rows + HALO, TILE), lambda i: (0, i)),
            spec((rows, TILE), lambda i: (0, i)),
            whole(rows, marks),
            spec((8, TILE), lambda i: (0, i)),
        ],
        [
            spec((rows, TILE), lambda i: (0, i)),
            spec((8, TILE), lambda i: (0, i)),
            spec((HALO, TILE), lambda i: (0, i)),
            spec((8, TILE), lambda i: (0, i)),
        ],
        [
            ((rows, MIXED), bf16),
            ((8, MIXED), f32),
            ((HALO, MIXED), f32),
            ((8, MIXED), f32),
        ],
        [
            pltpu.VMEM((TILE // LANES, rows + HALO, LANES), f32),
            pltpu.VMEM((3, rows, LANES), f32),
            pltpu.VMEM((CONV_WIDTH, TILE // LANES, rows + 8, LANES), f32),
        ],
        20,
    )(mixed_low, conv_out_grad, masks, taps)

    from_next = passed_along(rim, EVERY, -1)
    gate_grad, rim = lax.optimization_barrier((gate_grad, rim))
    gate_part = mm(gate_grad, gate_weight, NT)
    from_next, gate_part = lax.optimization_barrier((from_next, gate_part))
    fixed = jnp.concatenate([tail[: HALO - 8], tail[HALO - 8 :] + from_next], axis=0).astype(bf16)
    mixer_grad = lax.dynamic_update_slice(mixed_in_grad, fixed, (rows - HALO, 0))
    mixer_grad, rest_line = lax.optimization_barrier((mixer_grad, rest_line))
    rest_grad = lax.psum_scatter(rest_line, "head", scatter_dimension=0, tiled=True)
    rest_grad = lax.optimization_barrier(rest_grad).astype(f32)
    gate_weight_grad = jnp.concatenate([rest_grad[:own_rows], rest_grad[own_rows : 2 * own_rows]], axis=1)
    out_grad = rest_grad[2 * own_rows :]

    term = mm(normed, mixer_grad, TN).astype(bf16)
    line_rows = own_rows * lax.axis_size("head")

    def block_of(value, place, size):
        return lax.dynamic_slice_in_dim(value, place * size, size, axis=0)

    summed = []
    for k in range(chips):
        given = block_of(term, seq_index ^ (2 * k) ^ 1, line_rows)
        kept = block_of(term, seq_index ^ (2 * k), line_rows)
        summed.append(kept.astype(f32) + fetched(given, "seq", 1).astype(f32))
    sending = [part.astype(bf16) for part in summed[1:]]
    sending, mixer_grad = lax.optimization_barrier((sending, mixer_grad))
    line = summed[0]
    for k, part in enumerate(sending, 1):
        line = line + fetched(part, "seq", 2 * k).astype(f32)
    normed_in_grad = gate_part + mm(mixer_grad, mixer_weight, NT)
    norm_gain_grad = jnp.sum(normed_in_grad * inputs * in_scale, axis=0)
    scaled_in = normed_in_grad * norm_gain
    input_grad = (
        out_cotangent.astype(f32)
        + in_scale * scaled_in
        - inputs * in_scale**3 * jnp.mean(scaled_in * inputs, axis=-1, keepdims=True)
    )

    vector_local = jnp.concatenate(
        [
            norm_gain_grad,
            jnp.sum(middle_sums[:8], axis=0),
            tap_grads[: CONV_WIDTH + 1, :CONV_CHANNELS].reshape(-1),
            late_sums[1, :HEADS],
            late_sums[0, :HEADS] * rate_row[0, :HEADS],
            jnp.sum(middle_sums[8:].reshape(8, HEADS, HEAD_SIZE), axis=(0, 2)),
            jnp.zeros((-vector_params.shape[0] % count,), f32),
        ]
    )
    line, vector_local = lax.optimization_barrier((line, vector_local))
    parts = exchange(vector_local.reshape(count, -1))
    total = jnp.broadcast_to(jnp.sum(parts, axis=0, keepdims=True), parts.shape)
    vector_grad = exchange(total).reshape(-1)[: vector_params.shape[0]]
    mixer_weight_grad = block_of(line, head_index, own_rows)
    for k in range(1, lax.axis_size("head")):
        given = block_of(line, head_index ^ k, own_rows).astype(bf16)
        mixer_weight_grad = mixer_weight_grad + fetched(given, "head", k).astype(f32)

    in_grad = jnp.concatenate([gate_weight_grad, mixer_weight_grad[:, : CONV_CHANNELS + HEADS]], axis=1)
    in_first_new, in_second_new, in_weight_new = adamw(
        in_weight, in_first, in_second, in_grad, RATE_MATRIX, WEIGHT_DECAY
    )
    out_first_new, out_second_new, out_weight_new = adamw(
        out_weight, out_first, out_second, out_grad, RATE_MATRIX, WEIGHT_DECAY
    )
    vector_first_new, vector_second_new, vector_new = adamw(
        vector_params, vector_first, vector_second, vector_grad, RATE_VECTOR, 0.0
    )
    return (
        block_output,
        input_grad.astype(bf16),
        in_first_new,
        in_second_new,
        in_weight_new,
        out_first_new,
        out_second_new,
        out_weight_new,
        vector_first_new,
        vector_second_new,
        vector_new,
    )


def solution(mesh):
    split = P(EVERY, None)
    in_specs = (split, split, P(), split, split, P(), split, split, split, split, P(), P())
    out_specs = (split,) * 8 + (P(),) * 3
    return jax.shard_map(
        per_device, mesh=mesh, in_specs=in_specs, out_specs=out_specs, check_vma=False
    )
```

profile of v0, /device:TPU:0, one launch (start us, length us, event | category | flops | bytes accessed | tf_op | source)
XLA Modules:
  0.0 334.8 jit_solution(15807901261918226953)
XLA Ops:
  8.5 3.1 collective-permute-start
  11.6 2.6 collective-permute-start.1
  14.9 2.8 collective-permute-start.3
  22.3 2.7 collective-permute-start.4
  48.8 13.8 %shard_map.203 = (bf16[1024,1920]{1,0:T(8,128)(2,1)}, bf16[1040,1920]{1,0:T(8,128)(2,1)}, bf16[768,1920]{1,0:T(8,128)(2,1)}) custom-call(s32[1]{0:T(128)} %bitcast.6.where, bf16[1040,768]{1,0:T(8,128)(2,1)} %pad_maximum_fusion.2.normed, f32[1024,8]{1,0:T(8,128)} %copy.54.masks, f32[8,1920]{1,0:T(8,128)} %pad.20.taps, bf16[96,1920]{1,0:T(8,128)(2,1)} %copy-done.10, ...), custom_call_target="tpu_custom_call" | custom-call | bytes 47600000 | tf_op jit(solution)/shard_map/pallas_call | solution.py:617
  62.5 8.6 %shard_map.204 = (bf16[1024,1536]{1,0:T(8,128)(2,1)}, f32[1024,128]{1,0:T(8,128)}, f32[1024,128]{1,0:T(8,128)}, f32[4,32,256]{2,1,0:T(8,128)}, bf16[4,128,1536]{...) custom-call(bf16[1024,1920]{1,0:T(8,128)(2,1)} %get-tuple-element.104.values.both.raw, ...), custom_call_target="tpu_custom_call" | custom-call | bytes 30600000 | tf_op jit(solution)/shard_map/pallas_call | solution.py:647
  74.4 5.0 %all-to-all-start = ((bf16[32,50,128]{2,1,0:T(8,128)(2,1)}), bf16[32,50,128]{2,1,0:T(8,128)(2,1)}, u32[]{:S(2)}, u32[]{:S(2)}) async-start(bf16[32,50,128]{2,1,0:T(8,128)(2,1)} %pad_maximum_fusion.5), calls=%async_computation | async-start | bytes 917504 | tf_op jit(solution)/shard_map/all_to_all | solution.py:688
  81.5 12.9 %shard_map.205.diag = f32[1024,1536]{1,0:T(8,128)} custom-call(bf16[1024,1536]{1,0:T(8,128)(2,1)} %get-tuple-element.106.scaled, bf16[1024,1920]{1,0:T(8,128)(2,1)} %get-tuple-element.104.values.both.raw, f32[1024,128]{1,0:T(8,128)} %get-tuple-element.107.cumul, f32[4,32,256]{2,1,0:T(8,128)} %get-tuple-element.108.cumul_rows, f32[1024,8]{1,0:T(8,128)} %copy.54.masks, ...), custom_call_target="tpu_custom_call" | custom-call | bytes 54400000 | tf_op jit(solution)/shard_map/pallas_call | solution.py:707
  100.5 5.9 %all-to-all-start.1 = ((bf16[32,48,128]{2,1,0:T(8,128)(2,1)}), bf16[32,48,128]{2,1,0:T(8,128)(2,1)S(1)}, u32[]{:S(2)}, u32[]{:S(2)}) async-start(bf16[32,48,128]{2,1,0:T(8,128)(2,1)} %shard_map.206), calls=%async_computation.1 | async-start | bytes 786432 | tf_op jit(solution)/shard_map/all_to_all | solution.py:688
  106.5 5.2 %all-gather.2.cloned.1.call-done = bf16[3072,768]{1,0:T(8,128)(2,1)} async-done(((bf16[96,768]{1,0:T(8,128)(2,1)}), bf16[3072,768]{1,0:T(8,128)(2,1)}) %all-gather.2.cloned.1.call-update) | async-done | bytes 4718608 | tf_op jit(solution)/shard_map/all_gather | solution.py:611
  115.0 4.7 %fusion.11.gate = f32[1024,1536]{1,0:T(8,128)} fusion(bf16[1024,768]{1,0:T(8,128)(2,1)S(1)} %fusion.2, bf16[768,768]{1,0:T(8,128)(2,1)S(1)} %bitcast.66, bf16[768,768]{1,0:T(8,128)(2,1)S(1)} %bitcast.64), kind=kOutput, calls=%fused_computation.25 | convolution fusion | flops 2420637696 | bytes 10223616 | tf_op jit(solution)/shard_map/dot_general | solution.py:723
  121.8 4.5 %convolution_bitcast_fusion.normed_grad = f32[1024,1536]{1,0:T(8,128)} fusion(bf16[1536,768]{1,0:T(8,128)(2,1)S(1)} %bitcast.60, bf16[1024,768]{1,0:T(8,128)(2,1)S(1)} %copy-done.8), kind=kOutput, calls=%fused_computation.7 | convolution fusion | flops 2415919104 | bytes 10223616 | tf_op jit(solution)/shard_map/dot_general | solution.py:91
  127.1 24.8 %shard_map.207 = (bf16[1024,1536]{1,0:T(8,128)(2,1)}, bf16[1024,1536]{1,0:T(8,128)(2,1)}, bf16[1024,1536]{1,0:T(8,128)(2,1)}, f32[1024,128]{1,0:T(8,128)}, f32[1...) custom-call(f32[1024,1536]{1,0:T(8,128)} %shard_map.205.diag, ...), custom_call_target="tpu_custom_call" | custom-call | bytes 81600000 | tf_op jit(solution)/shard_map/pallas_call | solution.py:740
  151.8 3.7 %all-to-all-start.2 = ((bf16[32,48,128]{2,1,0:T(8,128)(2,1)}), bf16[32,48,128]{2,1,0:T(8,128)(2,1)S(1)}, u32[]{:S(2)}, u32[]{:S(2)}) async-start(bf16[32,48,128]{2,1,0:T(8,128)(2,1)} %bitcast.68), calls=%async_computation.2 | async-start | bytes 786432 | tf_op jit(solution)/shard_map/all_to_all | solution.py:688
  155.5 17.5 %shard_map.208 = (f32[1024,1536]{1,0:T(8,128)}, f32[1024,256]{1,0:T(8,128)}) custom-call(bf16[1024,1536]{1,0:T(8,128)(2,1)} %get-tuple-element.106.scaled, bf16[1024,1920]{1,0:T(8,128)(2,1)} %get-tuple-element.104.values.both.raw, f32[1024,128]{1,0:T(8,128)} %get-tuple-element.107.cumul, f32[4,32,256]{2,1,0:T(8,128)} %get-tuple-element.108.cumul_rows, ...), custom_call_target="tpu_custom_call" | custom-call | bytes 68000000 | tf_op jit(solution)/shard_map/pallas_call | solution.py:801
  175.8 4.7 %convolution_convert_fusion.1 = bf16[768,1536]{1,0:T(8,128)(2,1)S(1)} fusion(bf16[1024,768]{1,0:T(8,128)(2,1)S(1)} %fusion.2, bf16[1024,1536]{1,0:T(8,128)(2,1)} %get-tuple-element.137), kind=kOutput, calls=%fused_computation.9 | convolution fusion | flops 2417098752 | bytes 7077888 | tf_op jit(solution)/shard_map/dot_general | solution.py:91
  183.8 4.0 %convolution_convert_fusion = bf16[1536,768]{1,0:T(8,128)(2,1)} fusion(bf16[1024,1536]{1,0:T(8,128)(2,1)S(1)} %copy-done.35, bf16[1024,768]{1,0:T(8,128)(2,1)S(1)} %copy-done.9), kind=kOutput, calls=%fused_computation.8 | convolution fusion | flops 2417098752 | bytes 7077888 | tf_op jit(solution)/shard_map/dot_general | solution.py:91
  187.7 5.8 %all-to-all-start.3 = ((bf16[32,48,128]{2,1,0:T(8,128)(2,1)}), bf16[32,48,128]{2,1,0:T(8,128)(2,1)S(1)}, u32[]{:S(2)}, u32[]{:S(2)}) async-start(bf16[32,48,128]{2,1,0:T(8,128)(2,1)} %shard_map.209), calls=%async_computation.3 | async-start | bytes 786432 | tf_op jit(solution)/shard_map/all_to_all | solution.py:688
  193.7 4.4 %pad_maximum_fusion = bf16[32,96,768]{2,1,0:T(8,128)(2,1)} fusion(bf16[32,48,768]{2,1,0:T(8,128)(2,1)} %bitcast.62, bf16[32,24,768]{2,1,0:T(8,128)(2,1)} %bitcast.53, bf16[32,24,768]{2,1,0:T(8,128)(2,1)} %bitcast.52), kind=kLoop, calls=%fused_computation.6 | loop fusion | flops 14155776 | bytes 9437184 | tf_op jit(solution)/shard_map/concatenate | solution.py:830
  199.4 3.7 %fusion.3 = bf16[1024,768]{1,0:T(8,128)(2,1)} fusion(bf16[1024,768]{1,0:T(8,128)(2,1)S(1)} %copy-done, bf16[1024,1536]{1,0:T(8,128)(2,1)S(1)} %copy-done.36, bf16[1536,768]{1,0:T(8,128)(2,1)S(1)} %bitcast.61), kind=kOutput, calls=%fused_computation.14 | convolution fusion | flops 2418278400 | bytes 8650752 | tf_op jit(solution)/shard_map/dot_general | solution.py:91
  206.2 19.9 %shard_map.210 = (bf16[1024,1920]{1,0:T(8,128)(2,1)}, f32[8,128]{1,0:T(8,128)}) custom-call(bf16[1024,1920]{1,0:T(8,128)(2,1)} %get-tuple-element.104.values.both.raw, bf16[1024,1920]{1,0:T(8,128)(2,1)} %get-tuple-element.104.values.both.raw, f32[1024,128]{1,0:T(8,128)} %get-tuple-element.107.cumul, f32[1024,128]{1,0:T(8,128)} %get-tuple-element.127.delta, ...), custom_call_target="tpu_custom_call" | custom-call | bytes 61200000 | tf_op jit(solution)/shard_map/pallas_call | solution.py:842
  226.0 15.0 %shard_map.211 = (bf16[1024,1920]{1,0:T(8,128)(2,1)}, f32[8,1920]{1,0:T(8,128)}, f32[16,1920]{1,0:T(8,128)}, f32[8,1920]{1,0:T(8,128)}) custom-call(bf16[1040,1920]{1,0:T(8,128)(2,1)} %get-tuple-element.126.mixed, bf16[1024,1920]{1,0:T(8,128)(2,1)} %get-tuple-element.135.grad, f32[1024,8]{1,0:T(8,128)} %copy.54.masks, f32[8,1920]{1,0:T(8,128)} %pad.20.taps), custom_call_target="tpu_custom_call" | custom-call | bytes 68000000 | tf_op jit(solution)/shard_map/pallas_call | solution.py:885
  242.5 6.3 %fusion.10 = f32[1024,768]{1,0:T(8,128)} fusion(bf16[1024,1536]{1,0:T(8,128)(2,1)} %get-tuple-element.137, bf16[768,768]{1,0:T(8,128)(2,1)S(1)} %bitcast.67, bf16[768,768]{1,0:T(8,128)(2,1)S(1)} %bitcast.65), kind=kOutput, calls=%fused_computation.24 | convolution fusion | flops 2420637696 | bytes 8650752 | tf_op jit(solution)/shard_map/dot_general | solution.py:91
  249.5 9.3 %reduce-scatter.3.cloned.1.call-done = bf16[384,768]{1,0:T(8,128)(2,1)} async-done(((bf16[3072,768]{1,0:T(8,128)(2,1)}), bf16[384,768]{1,0:T(8,128)(2,1)}) %reduce-scatter.3.cloned.1.call-update) | async-done | bytes 589840 | tf_op jit(solution)/shard_map/reduce_scatter | solution.py:840
  258.8 5.8 %convolution_convert_fusion.2 = bf16[768,1920]{1,0:T(8,128)(2,1)S(1)} fusion(bf16[1024,768]{1,0:T(8,128)(2,1)S(1)} %fusion.2, bf16[1024,1920]{1,0:T(8,128)(2,1)} %maximum_dynamic-update-slice_fusion), kind=kOutput, calls=%fused_computation.10 | convolution fusion | flops 3021373440 | bytes 8454144 | tf_op jit(solution)/shard_map/dot_general | solution.py:91
  270.1 2.6 add_convert_fusion.1
  276.2 8.5 %fusion.9 = (f32[768]{0:T(1024)S(1)}, f32[1024]{0:T(1024)S(1)}, f32[1024,768]{1,0:T(8,128)}) fusion(bf16[1024,768]{1,0:T(8,128)(2,1)S(1)} %copy-done, f32[1024]{0:T(1024)S(1)} %copy-done.32, f32[1024,768]{1,0:T(8,128)S(1)} %copy-done.2, f32[768]{0:T(1024)S(1)} %slice.122, bf16[1024,1920]{1,0:T(8,128)(2,1)} %maximum_dynamic-update-slice_fusion, ...), kind=kOutput, calls=%fused_computation.20 | convolution fusion | flops 3026188544 | bytes 14759936 | tf_op jit(solution)/shard_map/dot_general | solution.py:91
  285.3 7.1 %collective-permute-done.18 = bf16[96,1920]{1,0:T(8,128)(2,1)} collective-permute-done((bf16[96,1920]{1,0:T(8,128)(2,1)S(1)}, bf16[96,1920]{1,0:T(8,128)(2,1)}, u32[]{:S(2)}, u32[]{:S(2)}) %collective-permute-start.18) | collective-permute-done | bytes 368672 | tf_op jit(solution)/shard_map/ppermute | solution.py:50
  299.2 4.6 %all-to-all-start.4 = ((f32[32,1,355]{2,1,0:T(1,128)}), f32[32,1,355]{2,1,0:T(1,128)S(1)}, u32[]{:S(2)}, u32[]{:S(2)}) async-start(f32[32,1,355]{2,1,0:T(1,128)} %all_to_all.26), calls=%async_computation.6 | async-start | bytes 98304 | tf_op jit(solution)/shard_map/all_to_all | solution.py:688
  303.8 4.9 %fusion.6 = bf16[1024,768]{1,0:T(8,128)(2,1)} fusion(bf16[1024,768]{1,0:T(8,128)(2,1)S(1)} %copy-done, bf16[1024,768]{1,0:T(8,128)(2,1)} %param.13, f32[1024]{0:T(1024)S(1)} %broadcast_multiply_fusion, f32[1024]{0:T(1024)S(1)} %copy-done.33, f32[768]{0:T(1024)S(1)} %slice.122, f32[1024]{0:T(1024)S(1)} %copy-done.32, f32[1024,768]{1,0:T(8,128)} %fusion.10, ...), kind=kLoop, calls=%fused_computation.17 | loop fusion | flops 7864320 | bytes 11025408 | tf_op jit(solution)/shard_map/convert_element_type | solution.py:983
  311.9 3.4 %all-to-all-start.5 = ((f32[32,1,355]{2,1,0:T(1,128)}), f32[32,1,355]{2,1,0:T(1,128)S(1)}, u32[]{:S(2)}, u32[]{:S(2)}) async-start(f32[32,1,355]{2,1,0:T(1,128)} %broadcast_in_dim.39), calls=%async_computation.7 | async-start | bytes 98304 | tf_op jit(solution)/shard_map/all_to_all | solution.py:688
  316.3 6.3 %all-to-all-done.5 = f32[32,1,355]{2,1,0:T(1,128)S(1)} async-done(((f32[32,1,355]{2,1,0:T(1,128)}), f32[32,1,355]{2,1,0:T(1,128)S(1)}, u32[]{:S(2)}, u32[]{:S(2)}) %all-to-all-start.5) | async-done | bytes 45472 | tf_op jit(solution)/shard_map/all_to_all | solution.py:688
  (225 shorter events, 86.3 us)
Async XLA Ops:
  7.2 22.7 %copy-start = (bf16[1024,768]{1,0:T(8,128)(2,1)S(1)}, bf16[1024,768]{1,0:T(8,128)(2,1)}, u32[]{:S(2)}) copy-start(bf16[1024,768]{1,0:T(8,128)(2,1)} %param.12) | copy-start | bytes 4718596
  7.2 104.4 %all-gather.2.cloned.1.call-start = ((), (), s32[]{:S(2)}) async-start(), calls=%async_computation.8 | async-start | bytes 4866048 | tf_op jit(solution)/shard_map/all_gather | solution.py:611
  8.5 13.1 %collective-permute-start = (bf16[24,1920]{1,0:T(8,128)(2,1)S(1)}, bf16[24,1920]{1,0:T(8,128)(2,1)S(1)}, u32[]{:S(2)}, u32[]{:S(2)}) collective-permute-start(bf16[24,1920]{1,0:T(8,128)(2,1)S(1)} %get-tuple-element.194), channel_id=1, source_target_pairs={{0,1},{1,0},{2,3},{3,2},{4,5},{5,4},{6,7},{7,6},{8,9},{9,8},{10,11... | collective-permute-start | bytes 276488 | tf_op jit(solution)/shard_map/ppermute | solution.py:50
  11.6 10.0 %collective-permute-start.1 = (bf16[24,1920]{1,0:T(8,128)(2,1)S(1)}, bf16[24,1920]{1,0:T(8,128)(2,1)S(1)}, u32[]{:S(2)}, u32[]{:S(2)}) collective-permute-start(bf16[24,1920]{1,0:T(8,128)(2,1)S(1)} %get-tuple-element.194), channel_id=1, source_target_pairs={{0,2},{1,3},{2,0},{3,1},{4,6},{5,7},{6,4},{7,5},{8,10},{9,11},{10,... | collective-permute-start | bytes 276488 | tf_op jit(solution)/shard_map/ppermute | solution.py:50
  14.1 7.4 %collective-permute-start.2 = (bf16[24,1920]{1,0:T(8,128)(2,1)S(1)}, bf16[24,1920]{1,0:T(8,128)(2,1)S(1)}, u32[]{:S(2)}, u32[]{:S(2)}) collective-permute-start(bf16[24,1920]{1,0:T(8,128)(2,1)S(1)} %get-tuple-element.194), channel_id=1, source_target_pairs={{0,3},{1,2},{2,1},{3,0},{4,7},{5,6},{6,5},{7,4},{8,11},{9,10},{10,... | collective-permute-start | bytes 276488 | tf_op jit(solution)/shard_map/ppermute | solution.py:50
  14.9 6.7 %collective-permute-start.3 = (bf16[16,768]{1,0:T(8,128)(2,1)S(1)}, bf16[16,768]{1,0:T(8,128)(2,1)S(1)}, u32[]{:S(2)}, u32[]{:S(2)}) collective-permute-start(bf16[16,768]{1,0:T(8,128)(2,1)S(1)} %slice.121), channel_id=1, source_target_pairs={{0,1},{1,2},{2,3},{3,4},{4,5},{5,6},{6,7},{7,8},{8,9},{9,10},{10,1... | collective-permute-start | bytes 73736 | tf_op jit(solution)/shard_map/ppermute | solution.py:46
  22.3 18.2 %collective-permute-start.4 = (bf16[96,1920]{1,0:T(8,128)(2,1)S(1)}, bf16[96,1920]{1,0:T(8,128)(2,1)}, u32[]{:S(2)}, u32[]{:S(2)}) collective-permute-start(bf16[96,1920]{1,0:T(8,128)(2,1)S(1)} %constant_dynamic-update-slice_fusion.others_0_), channel_id=1, source_target_pairs={{0,8},{4,12},{8,0},{12,4},{16,24},{20,28},{24,16},{28,20},{1,9},{5... | collective-permute-start | bytes 1105928 | tf_op jit(solution)/shard_map/ppermute | solution.py:50
  25.1 17.6 %collective-permute-start.5 = (bf16[96,1920]{1,0:T(8,128)(2,1)S(1)}, bf16[96,1920]{1,0:T(8,128)(2,1)}, u32[]{:S(2)}, u32[]{:S(2)}) collective-permute-start(bf16[96,1920]{1,0:T(8,128)(2,1)S(1)} %constant_dynamic-update-slice_fusion.others_0_), channel_id=1, source_target_pairs={{0,16},{4,20},{8,24},{12,28},{16,0},{20,4},{24,8},{28,12},{1,17},{... | collective-permute-start | bytes 1105928 | tf_op jit(solution)/shard_map/ppermute | solution.py:50
  26.6 16.1 %collective-permute-start.6 = (bf16[96,1920]{1,0:T(8,128)(2,1)S(1)}, bf16[96,1920]{1,0:T(8,128)(2,1)}, u32[]{:S(2)}, u32[]{:S(2)}) collective-permute-start(bf16[96,1920]{1,0:T(8,128)(2,1)S(1)} %constant_dynamic-update-slice_fusion.others_0_), channel_id=1, source_target_pairs={{0,24},{4,28},{8,16},{12,20},{16,8},{20,12},{24,0},{28,4},{1,25},{... | collective-permute-start | bytes 1105928 | tf_op jit(solution)/shard_map/ppermute | solution.py:50
  42.7 2.5 collective-permute-start.10
  42.7 2.9 collective-permute-start.7
  43.2 2.6 collective-permute-start.8
  43.2 3.0 collective-permute-start.9
  74.4 20.0 %all-to-all-start = ((bf16[32,50,128]{2,1,0:T(8,128)(2,1)}), bf16[32,50,128]{2,1,0:T(8,128)(2,1)}, u32[]{:S(2)}, u32[]{:S(2)}) async-start(bf16[32,50,128]{2,1,0:T(8,128)(2,1)} %pad_maximum_fusion.5), calls=%async_computation | async-start | bytes 917504 | tf_op jit(solution)/shard_map/all_to_all | solution.py:688
  100.5 25.8 %all-to-all-start.1 = ((bf16[32,48,128]{2,1,0:T(8,128)(2,1)}), bf16[32,48,128]{2,1,0:T(8,128)(2,1)S(1)}, u32[]{:S(2)}, u32[]{:S(2)}) async-start(bf16[32,48,128]{2,1,0:T(8,128)(2,1)} %shard_map.206), calls=%async_computation.1 | async-start | bytes 786432 | tf_op jit(solution)/shard_map/all_to_all | solution.py:688
  151.8 21.2 %all-to-all-start.2 = ((bf16[32,48,128]{2,1,0:T(8,128)(2,1)}), bf16[32,48,128]{2,1,0:T(8,128)(2,1)S(1)}, u32[]{:S(2)}, u32[]{:S(2)}) async-start(bf16[32,48,128]{2,1,0:T(8,128)(2,1)} %bitcast.68), calls=%async_computation.2 | async-start | bytes 786432 | tf_op jit(solution)/shard_map/all_to_all | solution.py:688
  187.7 17.7 %all-to-all-start.3 = ((bf16[32,48,128]{2,1,0:T(8,128)(2,1)}), bf16[32,48,128]{2,1,0:T(8,128)(2,1)S(1)}, u32[]{:S(2)}, u32[]{:S(2)}) async-start(bf16[32,48,128]{2,1,0:T(8,128)(2,1)} %shard_map.209), calls=%async_computation.3 | async-start | bytes 786432 | tf_op jit(solution)/shard_map/all_to_all | solution.py:688
  193.6 65.2 %reduce-scatter.3.cloned.1.call-start = ((), (), s32[]{:S(2)}) async-start(), calls=%async_computation.9 | async-start | bytes 5308416 | tf_op jit(solution)/shard_map/reduce_scatter | solution.py:840
  205.4 118.2 %reduce-scatter.5.cloned.1.call-start = ((), (), s32[]{:S(2)}) async-start(), calls=%async_computation.10 | async-start | bytes 737280 | tf_op jit(solution)/shard_map/reduce_scatter | solution.py:921
  241.1 7.8 %collective-permute-start.11 = (f32[8,1920]{1,0:T(8,128)}, f32[8,1920]{1,0:T(8,128)S(1)}, u32[]{:S(2)}, u32[]{:S(2)}) collective-permute-start(f32[8,1920]{1,0:T(8,128)} %get-tuple-element.136), channel_id=1, source_target_pairs={{1,0},{2,1},{3,2},{4,3},{5,4},{6,5},{7,6},{8,7},{9,8},{10,9},{11,1... | collective-permute-start | bytes 184328 | tf_op jit(solution)/shard_map/ppermute | solution.py:46
  266.3 3.8 %collective-permute-start.12 = (bf16[96,1920]{1,0:T(8,128)(2,1)S(1)}, bf16[96,1920]{1,0:T(8,128)(2,1)S(1)}, u32[]{:S(2)}, u32[]{:S(2)}) collective-permute-start(bf16[96,1920]{1,0:T(8,128)(2,1)S(1)} %get-tuple-element.177), channel_id=1, source_target_pairs={{0,4},{4,0},{8,12},{12,8},{16,20},{20,16},{24,28},{28,24},{1,5},{5... | collective-permute-start | bytes 1105928 | tf_op jit(solution)/shard_map/ppermute | solution.py:50
  266.4 3.7 %collective-permute-start.13 = (bf16[96,1920]{1,0:T(8,128)(2,1)S(1)}, bf16[96,1920]{1,0:T(8,128)(2,1)}, u32[]{:S(2)}, u32[]{:S(2)}) collective-permute-start(bf16[96,1920]{1,0:T(8,128)(2,1)S(1)} %get-tuple-element.176), channel_id=1, source_target_pairs={{0,4},{4,0},{8,12},{12,8},{16,20},{20,16},{24,28},{28,24},{1,5},{5... | collective-permute-start | bytes 1105928 | tf_op jit(solution)/shard_map/ppermute | solution.py:50
  266.9 3.2 collective-permute-start.14
  269.6 15.2 %collective-permute-start.15 = (bf16[96,1920]{1,0:T(8,128)(2,1)S(1)}, bf16[96,1920]{1,0:T(8,128)(2,1)}, u32[]{:S(2)}, u32[]{:S(2)}) collective-permute-start(bf16[96,1920]{1,0:T(8,128)(2,1)S(1)} %get-tuple-element.174), channel_id=1, source_target_pairs={{0,4},{4,0},{8,12},{12,8},{16,20},{20,16},{24,28},{28,24},{1,5},{5... | collective-permute-start | bytes 1105928 | tf_op jit(solution)/shard_map/ppermute | solution.py:50
  272.7 12.1 %collective-permute-start.16 = (bf16[96,1920]{1,0:T(8,128)(2,1)}, bf16[96,1920]{1,0:T(8,128)(2,1)S(1)}, u32[]{:S(2)}, u32[]{:S(2)}) collective-permute-start(bf16[96,1920]{1,0:T(8,128)(2,1)} %get-tuple-element.147), channel_id=1, source_target_pairs={{0,8},{4,12},{8,0},{12,4},{16,24},{20,28},{24,16},{28,20},{1,9},{5... | collective-permute-start | bytes 1105928 | tf_op jit(solution)/shard_map/ppermute | solution.py:50
  274.1 11.2 %collective-permute-start.17 = (bf16[96,1920]{1,0:T(8,128)(2,1)S(1)}, bf16[96,1920]{1,0:T(8,128)(2,1)S(1)}, u32[]{:S(2)}, u32[]{:S(2)}) collective-permute-start(bf16[96,1920]{1,0:T(8,128)(2,1)S(1)} %get-tuple-element.148), channel_id=1, source_target_pairs={{0,16},{4,20},{8,24},{12,28},{16,0},{20,4},{24,8},{28,12},{1,17},{... | collective-permute-start | bytes 1105928 | tf_op jit(solution)/shard_map/ppermute | solution.py:50
  274.7 17.7 %collective-permute-start.18 = (bf16[96,1920]{1,0:T(8,128)(2,1)S(1)}, bf16[96,1920]{1,0:T(8,128)(2,1)}, u32[]{:S(2)}, u32[]{:S(2)}) collective-permute-start(bf16[96,1920]{1,0:T(8,128)(2,1)S(1)} %get-tuple-element.149), channel_id=1, source_target_pairs={{0,24},{4,28},{8,16},{12,20},{16,8},{20,12},{24,0},{28,4},{1,25},{... | collective-permute-start | bytes 1105928 | tf_op jit(solution)/shard_map/ppermute | solution.py:50
  293.9 21.3 %collective-permute-start.19 = (bf16[24,1920]{1,0:T(8,128)(2,1)S(1)}, bf16[24,1920]{1,0:T(8,128)(2,1)}, u32[]{:S(2)}, u32[]{:S(2)}) collective-permute-start(bf16[24,1920]{1,0:T(8,128)(2,1)S(1)} %get-tuple-element.183), channel_id=1, source_target_pairs={{0,1},{1,0},{2,3},{3,2},{4,5},{5,4},{6,7},{7,6},{8,9},{9,8},{10,11... | collective-permute-start | bytes 276488 | tf_op jit(solution)/shard_map/ppermute | solution.py:50
  295.5 19.8 %collective-permute-start.20 = (bf16[24,1920]{1,0:T(8,128)(2,1)S(1)}, bf16[24,1920]{1,0:T(8,128)(2,1)}, u32[]{:S(2)}, u32[]{:S(2)}) collective-permute-start(bf16[24,1920]{1,0:T(8,128)(2,1)S(1)} %get-tuple-element.185), channel_id=1, source_target_pairs={{0,2},{1,3},{2,0},{3,1},{4,6},{5,7},{6,4},{7,5},{8,10},{9,11},{10,... | collective-permute-start | bytes 276488 | tf_op jit(solution)/shard_map/ppermute | solution.py:50
  297.9 17.4 %collective-permute-start.21 = (bf16[24,1920]{1,0:T(8,128)(2,1)S(1)}, bf16[24,1920]{1,0:T(8,128)(2,1)}, u32[]{:S(2)}, u32[]{:S(2)}) collective-permute-start(bf16[24,1920]{1,0:T(8,128)(2,1)S(1)} %get-tuple-element.184), channel_id=1, source_target_pairs={{0,3},{1,2},{2,1},{3,0},{4,7},{5,6},{6,5},{7,4},{8,11},{9,10},{10,... | collective-permute-start | bytes 276488 | tf_op jit(solution)/shard_map/ppermute | solution.py:50
  299.2 12.0 %all-to-all-start.4 = ((f32[32,1,355]{2,1,0:T(1,128)}), f32[32,1,355]{2,1,0:T(1,128)S(1)}, u32[]{:S(2)}, u32[]{:S(2)}) async-start(f32[32,1,355]{2,1,0:T(1,128)} %all_to_all.26), calls=%async_computation.6 | async-start | bytes 98304 | tf_op jit(solution)/shard_map/all_to_all | solution.py:688
  311.9 10.8 %all-to-all-start.5 = ((f32[32,1,355]{2,1,0:T(1,128)}), f32[32,1,355]{2,1,0:T(1,128)S(1)}, u32[]{:S(2)}, u32[]{:S(2)}) async-start(f32[32,1,355]{2,1,0:T(1,128)} %broadcast_in_dim.39), calls=%async_computation.7 | async-start | bytes 98304 | tf_op jit(solution)/shard_map/all_to_all | solution.py:688
  (38 other events, 366.3 us)
Sparse Core Ops, SparseCore 0:
  46.4 65.1 all-gather.1
  205.6 53.1 reduce-scatter.2
  270.2 21.9 reduce-scatter.4
where the time goes:
time: 337 us; the launch traced here: 335 us
  Pallas kernels  116 us (34%)
  starting transfers between devices  53.8 us (16%)
  matrix products  42.2 us (13%)
  other arithmetic  37.8 us (11%)
  waiting for transfers between devices  36.6 us (11%)
  local copies, waits for them, and re-layouts  33.4 us (10%)
  between operations  14.5 us (4%)
    dot_general x7, matrix products, mm(): lax.dot_general(left, right, (dims, ((), ())), preferred_element_type=f32...  37.5 us
    all_to_all x6, starting transfers between devices, exchange(): return lax.all_to_all(value, EVERY, split_axis=0, concat_axis=0, tiled=True)  28.4 us
    pallas_call x1, Pallas kernels, per_device(): call(middle, (stretches,), [by_block_r(INNER), spec((STRETCH, INNER), lam...  24.8 us
    ppermute x20, starting transfers between devices, fetched(): lax.ppermute(value, axis, [(k, k ^ bit) for k in range(lax.axis_size(axis...  20.9 us
    pallas_call x1, Pallas kernels, per_device(): call(late, (stretches,), [values_spec, both_spec, by_block(LANES), by_blo...  19.9 us
    pallas_call x1, Pallas kernels, per_device(): call(diagonal_back, (stretches,), [by_block(INNER), both_spec, by_block(L...  17.5 us
    pallas_call x1, Pallas kernels, per_device(): call(conv_back, (MIXED // TILE,), [spec((rows + HALO, TILE), lambda i: (0...  15 us
    pallas_call x1, Pallas kernels, per_device(): call(functools.partial(conv_forward, bits), (MIXED // TILE,), [pl.BlockSp...  13.8 us
  transfers between devices with their start and end apart: 31, of which 11 were waited for; matrix products, arithmetic and copies ran while one was open for 24% of the time, Pallas kernels for 27%

commit v1 on v0

--- a/solution.py
+++ b/solution.py
@@ -209,7 +209,7 @@
 def local_states(
     values, both, raw, masks, bias, rate, spreader,
     scaled, cumul_out, delta_out, cumul_rows, start, factors, device_state, device_decay,
-    state, reach, weighted, steps, ends,
+    state, reach, weighted, spreads,
 ):
     c = pl.program_id(0)
 
@@ -219,23 +219,24 @@
         reach[...] = jnp.ones_like(reach)
 
     delta = softplus(raw[...].astype(f32) + bias[...])
-    row = lax.broadcasted_iota(jnp.int32, (STRETCH, STRETCH), 0)
-    col = lax.broadcasted_iota(jnp.int32, (STRETCH, STRETCH), 1)
-    cumul = mm((row >= col).astype(f32), delta * rate[...], precision=HIGHEST)
+    cumul = sums_until(delta * rate[...], False)
     last = cumul[STRETCH - 1 : STRETCH, :]
     carry = jnp.exp(last) * masks[STRETCH - 1 : STRETCH, 4:5]
     cumul_out[...] = cumul
     delta_out[...] = delta
     cumul_rows[0] = cumul.T[: cumul_rows.shape[1], :] * LOG2E
-    steps[...] = spread_heads(delta, spreader[...])
-    ends[...] = spread_heads(jnp.exp(last - cumul) * masks[:, 3:4] * delta, spreader[...])
+    end_weight = jnp.exp(last - cumul) * masks[:, 3:4] * delta
+    line = lax.broadcasted_iota(jnp.int32, (8, LANES), 0)
+    factor_rows = jnp.where(line == 0, carry, reach[...])
+    spreads[...] = spread_heads(
+        jnp.concatenate([delta, end_weight, factor_rows, factor_rows], axis=0), spreader[...]
+    )
     for cols in tiles(INNER):
         v = values[:, cols].astype(f32)
-        scaled[:, cols] = (v * steps[:, cols]).astype(bf16)
-        weighted[:, cols] = (v * ends[:, cols]).astype(bf16)
+        scaled[:, cols] = (v * spreads[:STRETCH, cols]).astype(bf16)
+        weighted[:, cols] = (v * spreads[STRETCH : 2 * STRETCH, cols]).astype(bf16)
     start[0] = state[...].astype(bf16)
-    line = lax.broadcasted_iota(jnp.int32, (8, LANES), 0)
-    wide = spread_heads(jnp.where(line == 0, carry, reach[...]), spreader[...])
+    wide = spreads[2 * STRETCH : 2 * STRETCH + 8, :]
     factors[0] = wide
     state[...] = state[...] * wide[0:1, :] + mm(both[:, :STATE], weighted[...], TN)
     reach[...] = reach[...] * carry
@@ -244,7 +245,8 @@
     def _():
         for j, cols in enumerate(tiles(INNER)):
             device_state[j] = state[:, cols].astype(bf16)
-        device_decay[...] = reach[...]
+        top, low = in_two(reach[...])
+        device_decay[...] = jnp.concatenate([top[:1], low[:1], jnp.zeros((14, LANES), bf16)], axis=0)
 
 
 def spread_columns(cumul, columns):
@@ -331,22 +333,35 @@
     both_grad[:, STATE:] = mm(scores_grad, both[:, :STATE], TN)
 
 
-def prefix(parts, decays, second, out, reverse):
+def prefix(where, parts, decays, out, wide, reverse):
     count = parts.shape[0]
     rows = out.shape[1]
+    first = where[0] * rows // STATE
+    head = 2 * first + lax.broadcasted_iota(jnp.int32, (LANES, 2 * LANES), 1) // HEAD_SIZE
+    chosen = (lax.broadcasted_iota(jnp.int32, (LANES, 2 * LANES), 0) == head).astype(f32)
+    wide[...] = mm(decays[...], chosen, precision=HIGHEST)
+    places = where[0] * rows + lax.broadcasted_iota(jnp.int32, (rows, LANES), 0)
+    second = places >= (first + 1) * STATE
 
     def step(i, state):
         k = count - 1 - i if reverse else i
         out[pl.ds(k, 1)] = state.astype(bf16)[None]
-        two = decays[pl.ds(k, 1)][0]
-        decay = jnp.where(second[...] > 0.0, two[1:2, :], two[0:1, :])
+        two = wide[pl.ds(k, 1), :]
+        decay = jnp.where(second, two[:, LANES:], two[:, :LANES])
         return decay * state + parts[pl.ds(k, 1), :rows, :][0].astype(f32)
 
     lax.fori_loop(0, count, step, jnp.zeros((rows, LANES), f32))
 
 
-def head_sums(products, heads):
-    return sum(mm(product[...], heads[...]) for product in products)
+def sums_until(value, upper):
+    row = lax.broadcasted_iota(jnp.int32, (STRETCH, STRETCH), 0)
+    col = lax.broadcasted_iota(jnp.int32, (STRETCH, STRETCH), 1)
+    triangle = ((row <= col) if upper else (row >= col)).astype(bf16)
+    top = value.astype(bf16)
+    rest = value - top.astype(f32)
+    middle_part, low = in_two(rest)
+    out = mm(triangle, jnp.concatenate([top, middle_part, low], axis=1))
+    return out[:, :LANES] + out[:, LANES : 2 * LANES] + out[:, 2 * LANES :]
 
 
 def entered(start, factors, prior, j, cols):
@@ -357,7 +372,7 @@
     diag, values, both, cumul, masks, start, factors, prior, gate, normed_grad, gain, skip, heads,
     spreader,
     gated_low, gate_grad, mixed_grad, row_sums, reads_grad, after_local, sums, start_grad,
-    after_decay, full, entry, enter, gated_all, sig_all, mixed_all, entry_low, high, low, state_grad, tail_decay,
+    after_decay, full, entry, enter, gated_all, sig_all, mixed_all, entry_low, products, state_grad, tail_decay,
 ):
     i = pl.program_id(0)
 
@@ -406,12 +421,13 @@
             mixed_grad[rows, cols] = low_grad
             grad = low_grad.astype(f32)
             entry_low[rows, cols] = (grad * enter[rows, cols]).astype(bf16)
-            high[rows, cols], low[rows, cols] = in_two(grad * entry[rows, cols])
+            products[0, rows, cols], products[1, rows, cols] = in_two(grad * entry[rows, cols])
             sums[0:8, cols] += eights(back * unit)
             sums[8:16, cols] += eights(grad * values[rows, cols].astype(f32))
 
     chunks(STRETCH, CHUNK, rows_step)
-    row_sums[...] = head_sums((high, low), heads)
+    summed = mm(products[...].reshape(2 * STRETCH, INNER), heads[...])
+    row_sums[...] = summed[:STRETCH] + summed[STRETCH:]
     reads_grad[...] = mm(entry_low[...], full[...], NT)
     after_local[0] = state_grad[...].astype(bf16)
     after_decay[0] = tail_decay[...]
@@ -428,7 +444,7 @@
     values, both, cumul, delta, raw, masks, bias, rate, factors, start, prior, after_local, after_decay, after,
     diag_sums, scaled, out_grad, row_sums, reads_grad, both_grad, skip, heads, spreader,
     conv_grad, sums,
-    after_low, spread_grad, factor, wide, weighted, joint, outer_low, high, low,
+    after_low, spread_grad, spreads, weighted, products,
 ):
     @pl.when(pl.program_id(0) == 0)
     def _():
@@ -439,19 +455,20 @@
         here = after_local[0, :, cols].astype(f32) + after_decay[0, 0:1, cols] * after[j].astype(f32)
         after_low[:, cols] = here.astype(bf16)
         carry_rows.append(eights(here * entered(start, factors, prior, j, cols)) * factors[0, 0:1, cols])
-    carry_grad = sum(mm(part, heads[...]) for part in in_two(jnp.concatenate(carry_rows, axis=1)))
+    top, low = in_two(jnp.concatenate(carry_rows, axis=1))
+    products[4 * STRETCH :, :] = jnp.concatenate([top, low], axis=0)
     spread_grad[...] = mm(both[:, :STATE], after_low[...])
     step = delta[...]
     total = cumul[...]
     end_factor = jnp.exp(total[STRETCH - 1 : STRETCH, :] - total) * masks[:, 3:4]
-    factor[...] = spread_heads(end_factor, spreader[...])
-    wide[...] = spread_heads(step, spreader[...])
+    spreads[...] = spread_heads(jnp.concatenate([end_factor, step], axis=0), spreader[...])
+    later = lambda rows, k: pl.ds(pl.multiple_of(rows.start + k * STRETCH, CHUNK), CHUNK)
 
     def rows_step(rows):
         for cols in tiles(INNER):
             v = values[rows, cols].astype(f32)
-            ends = factor[rows, cols]
-            step_wide = wide[rows, cols]
+            ends = spreads[rows, cols]
+            step_wide = spreads[later(rows, 1), cols]
             inner = diag_sums[rows, cols]
             outer = spread_grad[rows, cols] * ends
             both_sums = inner + outer
@@ -459,22 +476,24 @@
                 step_wide * both_sums + skip[:, cols] * out_grad[rows, cols].astype(f32)
             ).astype(bf16)
             weighted[rows, cols] = (v * (ends * step_wide)).astype(bf16)
-            joint[rows, cols] = (v * both_sums).astype(bf16)
-            outer_low[rows, cols] = (v * outer).astype(bf16)
-            high[rows, cols], low[rows, cols] = in_two(scaled[rows, cols].astype(f32) * inner)
+            products[rows, cols] = (v * both_sums).astype(bf16)
+            products[later(rows, 1), cols] = (v * outer).astype(bf16)
+            top, low = in_two(scaled[rows, cols].astype(f32) * inner)
+            products[later(rows, 2), cols] = top
+            products[later(rows, 3), cols] = low
 
     chunks(STRETCH, CHUNK, rows_step)
     conv_grad[:, INNER : INNER + STATE] = (
         both_grad[:, :STATE] + mm(weighted[...], after_low[...], NT)
     ).astype(bf16)
     conv_grad[:, INNER + STATE : CONV_CHANNELS] = (both_grad[:, STATE:] + reads_grad[...]).astype(bf16)
-    end_spread = head_sums((outer_low,), heads) * step
-    last_grad = jnp.sum(end_spread, axis=0, keepdims=True) + jnp.sum(carry_grad, axis=0, keepdims=True)
-    cumul_grad = row_sums[...] - head_sums((high, low), heads) - end_spread
-    row = lax.broadcasted_iota(jnp.int32, (STRETCH, STRETCH), 0)
-    col = lax.broadcasted_iota(jnp.int32, (STRETCH, STRETCH), 1)
-    decay_grad = mm((row <= col).astype(f32), cumul_grad, precision=HIGHEST) + last_grad
-    step_grad = head_sums((joint,), heads) + decay_grad * rate[...]
+    summed = mm(products[...], heads[...])
+    joint, outer_sum, top, low = [summed[k * STRETCH : (k + 1) * STRETCH] for k in range(4)]
+    end_spread = outer_sum * step
+    last_grad = jnp.sum(end_spread, axis=0, keepdims=True) + jnp.sum(summed[4 * STRETCH :], axis=0, keepdims=True)
+    cumul_grad = row_sums[...] - (top + low) - end_spread
+    decay_grad = sums_until(cumul_grad, True) + last_grad
+    step_grad = joint + decay_grad * rate[...]
     pre_grad = step_grad * sigmoid(raw[...].astype(f32) + bias[...])
     conv_grad[:, CONV_CHANNELS:] = pre_grad.astype(bf16)
     sums[0:1, :] += jnp.sum(decay_grad * step, axis=0, keepdims=True)
@@ -604,10 +623,10 @@
     near, extended, normed, masks, taps, spreader, head_of = lax.optimization_barrier(
         ([piece for _, piece in near], extended, normed, masks, taps, spreader, head_of)
     )
+    rest_own = jnp.concatenate([in_weight[:, :WIDTH], in_weight[:, WIDTH:INNER], out_weight], axis=0).astype(bf16)
+    rest_own, _ = lax.optimization_barrier((rest_own, mixer_group))
     bits = [2 * k for k in range(chips)] + [2 * k + 1 for k in range(chips)]
     pieces = near + [fetched(piece, "seq", 1) for piece in near]
-    rest_own = jnp.concatenate([in_weight[:, :WIDTH], in_weight[:, WIDTH:INNER], out_weight], axis=0).astype(bf16)
-    rest_own, pieces = lax.optimization_barrier((rest_own, pieces))
     rest = lax.all_gather(rest_own, EVERY, axis=0, tiled=True).reshape(count, -1, WIDTH)
     gate_weight = jnp.concatenate(
         [rest[:, :own_rows].reshape(WIDTH, WIDTH), rest[:, own_rows : 2 * own_rows].reshape(WIDTH, WIDTH)], axis=1
@@ -656,7 +675,7 @@
             per_block(STATE, INNER),
             per_block(8, INNER),
             whole(PAIRS, STATE, LANES),
-            whole(8, LANES),
+            whole(16, LANES),
         ],
         [
             ((rows, INNER), bf16),
@@ -666,22 +685,19 @@
             ((stretches, STATE, INNER), bf16),
             ((stretches, 8, INNER), f32),
             ((PAIRS, STATE, LANES), bf16),
-            ((8, LANES), f32),
+            ((16, LANES), bf16),
         ],
         [
             pltpu.VMEM((STATE, INNER), f32),
             pltpu.VMEM((8, LANES), f32),
             pltpu.VMEM((STRETCH, INNER), bf16),
-            pltpu.VMEM((STRETCH, INNER), f32),
-            pltpu.VMEM((STRETCH, INNER), f32),
+            pltpu.VMEM((2 * STRETCH + 16, INNER), f32),
         ],
         9,
     )(convolved, convolved, convolved, masks, bias_row, rate_row, spreader)
 
     share = PAIRS * STATE // count
-    decay_high = device_decay[0].astype(bf16)
-    decay_low = (device_decay[0] - decay_high.astype(f32)).astype(bf16)
-    decay_rows = jnp.broadcast_to(jnp.stack([decay_high, decay_low])[None], (count, 2, LANES))
+    decay_rows = jnp.broadcast_to(device_decay[None, :2], (count, 2, LANES))
     sent = jnp.concatenate([device_state.reshape(count, share, LANES), decay_rows], axis=1)
 
     def exchange(value):
@@ -690,18 +706,14 @@
     def scan_parts(parts, reverse):
         return pl.pallas_call(
             functools.partial(prefix, reverse=reverse),
+            in_specs=[pl.BlockSpec(memory_space=pltpu.SMEM)] + [pl.BlockSpec(memory_space=pltpu.VMEM)] * 2,
             out_shape=jax.ShapeDtypeStruct((count, share, LANES), bf16),
+            scratch_shapes=[pltpu.VMEM((count, 2 * LANES), f32)],
             compiler_params=pltpu.CompilerParams(vmem_limit_bytes=ROOM),
-        )(parts, pair_decays, second)
+        )(device_index.reshape(1), parts, all_decays)
 
     arrived = exchange(sent)
-    all_decays = arrived[:, share, :HEADS].astype(f32) + arrived[:, share + 1, :HEADS].astype(f32)
-    wide_decays = jnp.repeat(all_decays, HEAD_SIZE, axis=1).reshape(count, PAIRS, LANES)
-    wide_decays = jnp.pad(wide_decays, ((0, 0), (0, 1), (0, 0)))
-    first_pair = device_index * share // STATE
-    pair_decays = lax.dynamic_slice_in_dim(wide_decays, first_pair, 2, axis=1)
-    places = device_index * share + lax.broadcasted_iota(jnp.int32, (share, LANES), 0)
-    second = (places >= (first_pair + 1) * STATE).astype(f32)
+    all_decays = arrived[:, share].astype(f32) + arrived[:, share + 1].astype(f32)
     prior = exchange(scan_parts(arrived, False)).reshape(PAIRS, STATE, LANES)
 
     diag = call(
@@ -786,8 +798,7 @@
             wide_scratch(f32),
             wide_scratch(bf16),
             wide_scratch(bf16),
-            wide_scratch(bf16),
-            wide_scratch(bf16),
+            pltpu.VMEM((2, STRETCH, INNER), bf16),
             pltpu.VMEM((STATE, INNER), f32),
             pltpu.VMEM((8, INNER), f32),
         ],
@@ -872,10 +883,10 @@
         [
             pltpu.VMEM((STATE, INNER), bf16),
             wide_scratch(f32),
-            wide_scratch(f32),
-            wide_scratch(f32),
-        ]
-        + [wide_scratch(bf16)] * 5,
+            pltpu.VMEM((2 * STRETCH, INNER), f32),
+            wide_scratch(bf16),
+            pltpu.VMEM((4 * STRETCH + 16, INNER), bf16),
+        ],
         18,
     )(
         convolved, convolved, cumul, delta, convolved, masks, bias_row, rate_row, factors, start, prior, after_local, after_decay,
@@ -917,12 +928,6 @@
     from_next, gate_part = lax.optimization_barrier((from_next, gate_part))
     fixed = jnp.concatenate([tail[: HALO - 8], tail[HALO - 8 :] + from_next], axis=0).astype(bf16)
     mixer_grad = lax.dynamic_update_slice(mixed_in_grad, fixed, (rows - HALO, 0))
-    mixer_grad, rest_line = lax.optimization_barrier((mixer_grad, rest_line))
-    rest_grad = lax.psum_scatter(rest_line, "head", scatter_dimension=0, tiled=True)
-    rest_grad = lax.optimization_barrier(rest_grad).astype(f32)
-    gate_weight_grad = jnp.concatenate([rest_grad[:own_rows], rest_grad[own_rows : 2 * own_rows]], axis=1)
-    out_grad = rest_grad[2 * own_rows :]
-
     term = mm(normed, mixer_grad, TN).astype(bf16)
     line_rows = own_rows * lax.axis_size("head")
 
@@ -935,7 +940,22 @@
         kept = block_of(term, seq_index ^ (2 * k), line_rows)
         summed.append(kept.astype(f32) + fetched(given, "seq", 1).astype(f32))
     sending = [part.astype(bf16) for part in summed[1:]]
-    sending, mixer_grad = lax.optimization_barrier((sending, mixer_grad))
+    early = jnp.concatenate(
+        [
+            jnp.sum(middle_sums[:8], axis=0),
+            tap_grads[: CONV_WIDTH + 1, :CONV_CHANNELS].reshape(-1),
+            late_sums[1, :HEADS],
+            late_sums[0, :HEADS] * rate_row[0, :HEADS],
+            jnp.sum(middle_sums[8:].reshape(8, HEADS, HEAD_SIZE), axis=(0, 2)),
+        ]
+    )
+    size = early.shape[0]
+    early = jnp.pad(early, (0, -size % count)).reshape(count, -1)
+    sending, mixer_grad, rest_line, early = lax.optimization_barrier((sending, mixer_grad, rest_line, early))
+    rest_grad = lax.psum_scatter(rest_line, "head", scatter_dimension=0, tiled=True)
+    rest_grad = lax.optimization_barrier(rest_grad).astype(f32)
+    gate_weight_grad = jnp.concatenate([rest_grad[:own_rows], rest_grad[own_rows : 2 * own_rows]], axis=1)
+    out_grad = rest_grad[2 * own_rows :]
     line = summed[0]
     for k, part in enumerate(sending, 1):
         line = line + fetched(part, "seq", 2 * k).astype(f32)
@@ -948,21 +968,17 @@
         - inputs * in_scale**3 * jnp.mean(scaled_in * inputs, axis=-1, keepdims=True)
     )
 
-    vector_local = jnp.concatenate(
-        [
-            norm_gain_grad,
-            jnp.sum(middle_sums[:8], axis=0),
-            tap_grads[: CONV_WIDTH + 1, :CONV_CHANNELS].reshape(-1),
-            late_sums[1, :HEADS],
-            late_sums[0, :HEADS] * rate_row[0, :HEADS],
-            jnp.sum(middle_sums[8:].reshape(8, HEADS, HEAD_SIZE), axis=(0, 2)),
-            jnp.zeros((-vector_params.shape[0] % count,), f32),
+    early_parts = exchange(early)
+    line, norm_gain_grad, early_parts = lax.optimization_barrier((line, norm_gain_grad, early_parts))
+    own_early = jnp.sum(early_parts, axis=0)
+    both_vectors = jnp.concatenate([own_early, norm_gain_grad])
+    both_vectors = exchange(jnp.broadcast_to(both_vectors[None], (count,) + both_vectors.shape))
+    vector_grad = jnp.concatenate(
+        [
+            jnp.sum(both_vectors[:, own_early.shape[0] :], axis=0),
+            both_vectors[:, : own_early.shape[0]].reshape(-1)[:size],
         ]
     )
-    line, vector_local = lax.optimization_barrier((line, vector_local))
-    parts = exchange(vector_local.reshape(count, -1))
-    total = jnp.broadcast_to(jnp.sum(parts, axis=0, keepdims=True), parts.shape)
-    vector_grad = exchange(total).reshape(-1)[: vector_params.shape[0]]
     mixer_weight_grad = block_of(line, head_index, own_rows)
     for k in range(1, lax.axis_size("head")):
         given = block_of(line, head_index ^ k, own_rows).astype(bf16)

time: 337 us -> 311 us (0.923)
  waiting for transfers between devices: 36.6 us -> 27.6 us
  local copies, waits for them, and re-layouts: 33.4 us -> 27.1 us
  other arithmetic: 37.8 us -> 32.1 us
    reduce_scatter x1, waiting for transfers between devices: 9.28 us -> 0.02 us  [per_device(): lax.psum_scatter(rest_term, 'seq', scatter_dimension=0, tiled=True)]
    all_gather x1, waiting for transfers between devices: 5.18 us -> 0.02 us  [per_device(): lax.all_gather(rest_own, EVERY, axis=0, tiled=True)]
    ppermute x20, waiting for transfers between devices: 10.9 us -> 15 us  [fetched(): lax.ppermute(value, axis, [(k, k ^ bit) for k in range(lax.axis_size(axis...]
    all_to_all x6, starting transfers between devices: 28.4 us -> 24.8 us  [exchange(): return lax.all_to_all(value, EVERY, split_axis=0, concat_axis=0, tiled=True)]
  transfers between devices with their start and end apart: 31 -> 31, of which waited for: 11 -> 12; matrix products, arithmetic and copies ran while one was open for 24% -> 23% of each run, Pallas kernels for 27% -> 29%
where the time goes in v1:
time: 311 us; the launch traced here: 310 us
  Pallas kernels  116 us (37%)
  starting transfers between devices  53.3 us (17%)
  matrix products  39.5 us (13%)
  other arithmetic  32.1 us (10%)
  waiting for transfers between devices  27.6 us (9%)
  local copies, waits for them, and re-layouts  27.1 us (9%)
  between operations  14.6 us (5%)
    dot_general x7, matrix products, mm(): lax.dot_general(left, right, (dims, ((), ())), preferred_element_type=f32...  34.8 us
    all_to_all x6, starting transfers between devices, exchange(): return lax.all_to_all(value, EVERY, split_axis=0, concat_axis=0, tiled=True)  24.8 us
    pallas_call x1, Pallas kernels, per_device(): call(middle, (stretches,), [by_block_r(INNER), spec((STRETCH, INNER), lam...  24.1 us
    ppermute x20, starting transfers between devices, fetched(): lax.ppermute(value, axis, [(k, k ^ bit) for k in range(lax.axis_size(axis...  23.5 us
    pallas_call x1, Pallas kernels, per_device(): call(late, (stretches,), [values_spec, both_spec, by_block(LANES), by_blo...  19.8 us
    pallas_call x1, Pallas kernels, per_device(): call(diagonal_back, (stretches,), [by_block(INNER), both_spec, by_block(L...  17.5 us
    ppermute x20, waiting for transfers between devices, fetched(): lax.ppermute(value, axis, [(k, k ^ bit) for k in range(lax.axis_size(axis...  15 us
    pallas_call x1, Pallas kernels, per_device(): call(conv_back, (MIXED // TILE,), [spec((rows + HALO, TILE), lambda i: (0...  15 us
  transfers between devices with their start and end apart: 31, of which 12 were waited for; matrix products, arithmetic and copies ran while one was open for 23% of the time, Pallas kernels for 29%

profile of v1, /device:TPU:0, one launch (start us, length us, event | category | flops | bytes accessed | tf_op | source)
XLA Modules:
  0.0 309.7 jit_solution(14757291073881063308)
XLA Ops:
  8.5 3.1 collective-permute-start
  11.5 2.6 collective-permute-start.1
  14.9 2.8 collective-permute-start.3
  25.4 2.9 collective-permute-start.4
  40.9 6.1 %collective-permute-done.5.others_2_ = bf16[96,1920]{1,0:T(8,128)(2,1)} collective-permute-done((bf16[96,1920]{1,0:T(8,128)(2,1)S(1)}, bf16[96,1920]{1,0:T(8,128)(2,1)}, u32[]{:S(2)}, u32[]{:S(2)}) %collective-permute-start.5) | collective-permute-done | bytes 368672 | tf_op jit(solution)/shard_map/ppermute | solution.py:50
  50.6 13.8 %shard_map.203 = (bf16[1024,1920]{1,0:T(8,128)(2,1)}, bf16[1040,1920]{1,0:T(8,128)(2,1)}, bf16[768,1920]{1,0:T(8,128)(2,1)}) custom-call(s32[1]{0:T(128)} %bitcast.6.where, bf16[1040,768]{1,0:T(8,128)(2,1)} %pad_maximum_fusion.2.normed, f32[1024,8]{1,0:T(8,128)} %copy.63.masks, f32[8,1920]{1,0:T(8,128)} %pad.20.taps, bf16[96,1920]{1,0:T(8,128)(2,1)} %copy-done.11, ...), custom_call_target="tpu_custom_call" | custom-call | bytes 47600000 | tf_op jit(solution)/shard_map/pallas_call | solution.py:636
  64.4 8.0 %shard_map.204 = (bf16[1024,1536]{1,0:T(8,128)(2,1)}, f32[1024,128]{1,0:T(8,128)}, f32[1024,128]{1,0:T(8,128)}, f32[4,32,256]{2,1,0:T(8,128)}, bf16[4,128,1536]{...) custom-call(bf16[1024,1920]{1,0:T(8,128)(2,1)} %get-tuple-element.89.values.both., ...), custom_call_target="tpu_custom_call" | custom-call | bytes 30600000 | tf_op jit(solution)/shard_map/pallas_call | solution.py:666
  75.0 3.3 %all-to-all-start = ((bf16[32,50,128]{2,1,0:T(8,128)(2,1)}), bf16[32,50,128]{2,1,0:T(8,128)(2,1)}, u32[]{:S(2)}, u32[]{:S(2)}) async-start(bf16[32,50,128]{2,1,0:T(8,128)(2,1)} %pad_maximum_fusion.5), calls=%async_computation | async-start | bytes 917504 | tf_op jit(solution)/shard_map/all_to_all | solution.py:704
  80.3 12.9 %shard_map.205.diag = f32[1024,1536]{1,0:T(8,128)} custom-call(bf16[1024,1536]{1,0:T(8,128)(2,1)} %get-tuple-element.91.scaled, bf16[1024,1920]{1,0:T(8,128)(2,1)} %get-tuple-element.89.values.both.raw, f32[1024,128]{1,0:T(8,128)} %get-tuple-element.92.cumul, f32[4,32,256]{2,1,0:T(8,128)} %get-tuple-element.93.cumul_rows, f32[1024,8]{1,0:T(8,128)} %copy.63.masks, ...), custom_call_target="tpu_custom_call" | custom-call | bytes 54400000 | tf_op jit(solution)/shard_map/pallas_call | solution.py:719
  98.4 4.5 %all-to-all-start.1 = ((bf16[32,48,128]{2,1,0:T(8,128)(2,1)}), bf16[32,48,128]{2,1,0:T(8,128)(2,1)S(1)}, u32[]{:S(2)}, u32[]{:S(2)}) async-start(bf16[32,48,128]{2,1,0:T(8,128)(2,1)} %shard_map.206), calls=%async_computation.1 | async-start | bytes 786432 | tf_op jit(solution)/shard_map/all_to_all | solution.py:704
  106.3 4.7 %fusion.11.gate = f32[1024,1536]{1,0:T(8,128)} fusion(bf16[1024,768]{1,0:T(8,128)(2,1)S(1)} %fusion.2, bf16[768,768]{1,0:T(8,128)(2,1)S(1)} %bitcast.75, bf16[768,768]{1,0:T(8,128)(2,1)S(1)} %bitcast.73), kind=kOutput, calls=%fused_computation.25 | convolution fusion | flops 2420637696 | bytes 10223616 | tf_op jit(solution)/shard_map/dot_general | solution.py:735
  113.2 4.5 %convolution_bitcast_fusion.normed_grad = f32[1024,1536]{1,0:T(8,128)} fusion(bf16[1536,768]{1,0:T(8,128)(2,1)S(1)} %bitcast.69, bf16[1024,768]{1,0:T(8,128)(2,1)S(1)} %copy-done.8), kind=kOutput, calls=%fused_computation.7 | convolution fusion | flops 2415919104 | bytes 10223616 | tf_op jit(solution)/shard_map/dot_general | solution.py:91
  118.4 24.1 %shard_map.207 = (bf16[1024,1536]{1,0:T(8,128)(2,1)}, bf16[1024,1536]{1,0:T(8,128)(2,1)}, bf16[1024,1536]{1,0:T(8,128)(2,1)}, f32[1024,128]{1,0:T(8,128)}, f32[1...) custom-call(f32[1024,1536]{1,0:T(8,128)} %shard_map.205.diag, ...), custom_call_target="tpu_custom_call" | custom-call | bytes 81600000 | tf_op jit(solution)/shard_map/pallas_call | solution.py:752
  142.5 5.7 %all-to-all-start.2 = ((bf16[32,48,128]{2,1,0:T(8,128)(2,1)}), bf16[32,48,128]{2,1,0:T(8,128)(2,1)S(1)}, u32[]{:S(2)}, u32[]{:S(2)}) async-start(bf16[32,48,128]{2,1,0:T(8,128)(2,1)} %bitcast.79), calls=%async_computation.2 | async-start | bytes 786432 | tf_op jit(solution)/shard_map/all_to_all | solution.py:704
  148.2 17.5 %shard_map.208 = (f32[1024,1536]{1,0:T(8,128)}, f32[1024,256]{1,0:T(8,128)}) custom-call(bf16[1024,1536]{1,0:T(8,128)(2,1)} %get-tuple-element.91.scaled, bf16[1024,1920]{1,0:T(8,128)(2,1)} %get-tuple-element.89.values.both.raw, f32[1024,128]{1,0:T(8,128)} %get-tuple-element.92.cumul, f32[4,32,256]{2,1,0:T(8,128)} %get-tuple-element.93.cumul_rows, ...), custom_call_target="tpu_custom_call" | custom-call | bytes 68000000 | tf_op jit(solution)/shard_map/pallas_call | solution.py:812
  168.7 4.7 %convolution_convert_fusion.1 = bf16[768,1536]{1,0:T(8,128)(2,1)S(1)} fusion(bf16[1024,768]{1,0:T(8,128)(2,1)S(1)} %fusion.2, bf16[1024,1536]{1,0:T(8,128)(2,1)} %get-tuple-element.122), kind=kOutput, calls=%fused_computation.9 | convolution fusion | flops 2417098752 | bytes 7077888 | tf_op jit(solution)/shard_map/dot_general | solution.py:91
  176.6 3.9 %convolution_convert_fusion = bf16[1536,768]{1,0:T(8,128)(2,1)} fusion(bf16[1024,1536]{1,0:T(8,128)(2,1)S(1)} %copy-done.34, bf16[1024,768]{1,0:T(8,128)(2,1)S(1)} %copy-done.9), kind=kOutput, calls=%fused_computation.8 | convolution fusion | flops 2417098752 | bytes 7077888 | tf_op jit(solution)/shard_map/dot_general | solution.py:91
  180.6 5.8 %all-to-all-start.3 = ((bf16[32,48,128]{2,1,0:T(8,128)(2,1)}), bf16[32,48,128]{2,1,0:T(8,128)(2,1)S(1)}, u32[]{:S(2)}, u32[]{:S(2)}) async-start(bf16[32,48,128]{2,1,0:T(8,128)(2,1)} %shard_map.209), calls=%async_computation.3 | async-start | bytes 786432 | tf_op jit(solution)/shard_map/all_to_all | solution.py:704
  186.7 4.4 %pad_maximum_fusion = bf16[32,96,768]{2,1,0:T(8,128)(2,1)} fusion(bf16[32,48,768]{2,1,0:T(8,128)(2,1)} %bitcast.71, bf16[32,24,768]{2,1,0:T(8,128)(2,1)} %bitcast.62, bf16[32,24,768]{2,1,0:T(8,128)(2,1)} %bitcast.61), kind=kLoop, calls=%fused_computation.6 | loop fusion | flops 14155776 | bytes 9437184 | tf_op jit(solution)/shard_map/concatenate | solution.py:841
  192.4 3.7 %fusion.3 = bf16[1024,768]{1,0:T(8,128)(2,1)} fusion(bf16[1024,768]{1,0:T(8,128)(2,1)S(1)} %copy-done, bf16[1024,1536]{1,0:T(8,128)(2,1)S(1)} %copy-done.35, bf16[1536,768]{1,0:T(8,128)(2,1)S(1)} %bitcast.70), kind=kOutput, calls=%fused_computation.14 | convolution fusion | flops 2418278400 | bytes 8650752 | tf_op jit(solution)/shard_map/dot_general | solution.py:91
  199.0 19.8 %shard_map.210 = (bf16[1024,1920]{1,0:T(8,128)(2,1)}, f32[8,128]{1,0:T(8,128)}) custom-call(bf16[1024,1920]{1,0:T(8,128)(2,1)} %get-tuple-element.89.values.both.raw, bf16[1024,1920]{1,0:T(8,128)(2,1)} %get-tuple-element.89.values.both.raw, f32[1024,128]{1,0:T(8,128)} %get-tuple-element.92.cumul, f32[1024,128]{1,0:T(8,128)} %get-tuple-element.112.delta, ...), custom_call_target="tpu_custom_call" | custom-call | bytes 61200000 | tf_op jit(solution)/shard_map/pallas_call | solution.py:853
  218.8 15.0 %shard_map.211 = (bf16[1024,1920]{1,0:T(8,128)(2,1)}, f32[8,1920]{1,0:T(8,128)}, f32[16,1920]{1,0:T(8,128)}, f32[8,1920]{1,0:T(8,128)}) custom-call(bf16[1040,1920]{1,0:T(8,128)(2,1)} %get-tuple-element.111.mixed, bf16[1024,1920]{1,0:T(8,128)(2,1)} %get-tuple-element.120.grad, f32[1024,8]{1,0:T(8,128)} %copy.63.masks, f32[8,1920]{1,0:T(8,128)} %pad.20.taps), custom_call_target="tpu_custom_call" | custom-call | bytes 68000000 | tf_op jit(solution)/shard_map/pallas_call | solution.py:896
  235.4 6.3 %fusion.10 = f32[1024,768]{1,0:T(8,128)} fusion(bf16[1024,1536]{1,0:T(8,128)(2,1)} %get-tuple-element.122, bf16[768,768]{1,0:T(8,128)(2,1)S(1)} %bitcast.76, bf16[768,768]{1,0:T(8,128)(2,1)S(1)} %bitcast.74), kind=kOutput, calls=%fused_computation.24 | convolution fusion | flops 2420637696 | bytes 8650752 | tf_op jit(solution)/shard_map/dot_general | solution.py:91
  241.8 3.7 %convolution_convert_fusion.2 = bf16[768,1920]{1,0:T(8,128)(2,1)S(1)} fusion(bf16[1024,768]{1,0:T(8,128)(2,1)S(1)} %fusion.2, bf16[1024,1920]{1,0:T(8,128)(2,1)S(1)} %maximum_dynamic-update-slice_fusion), kind=kOutput, calls=%fused_computation.10 | convolution fusion | flops 3021373440 | bytes 8454144 | tf_op jit(solution)/shard_map/dot_general | solution.py:91
  247.2 2.8 collective-permute-start.12
  258.6 2.6 all-to-all-start.4
  262.0 7.9 %fusion.9 = (f32[768]{0:T(1024)S(1)}, f32[1024]{0:T(1024)S(1)}, f32[1024,768]{1,0:T(8,128)S(1)}) fusion(bf16[1024,768]{1,0:T(8,128)(2,1)S(1)} %copy-done, f32[1024]{0:T(1024)S(1)} %copy-done.27, f32[1024,768]{1,0:T(8,128)} %fusion.10, f32[768]{0:T(1024)S(1)} %slice.127, bf16[1024,1920]{1,0:T(8,128)(2,1)} %copy-done.33, bf16[768,1920]{1,0:T(8,128)(2,1)} %get-tuple-element.132), kind=kOutput, calls=%fused_computation.20 | convolution fusion | flops 3026188544 | bytes 14759936 | tf_op jit(solution)/shard_map/dot_general | solution.py:91
  272.1 2.9 all-to-all-done.4
  278.2 3.1 %collective-permute-start.21 = (bf16[24,1920]{1,0:T(8,128)(2,1)S(1)}, bf16[24,1920]{1,0:T(8,128)(2,1)S(1)}, u32[]{:S(2)}, u32[]{:S(2)}) collective-permute-start(bf16[24,1920]{1,0:T(8,128)(2,1)S(1)} %get-tuple-element.170), channel_id=1, source_target_pairs={{0,3},{1,2},{2,1},{3,0},{4,7},{5,6},{6,5},{7,4},{8,11},{9,10},{10,... | collective-permute-start | bytes 276488 | tf_op jit(solution)/shard_map/ppermute | solution.py:50
  282.1 2.9 all-to-all-start.5
  286.9 2.9 collective-permute-done.20
  291.2 5.5 %all-to-all-done.5 = f32[32,1,1099]{2,1,0:T(1,128)S(1)} async-done(((f32[32,1,1099]{2,1,0:T(1,128)}), f32[32,1,1099]{2,1,0:T(1,128)S(1)}, u32[]{:S(2)}, u32[]{:S(2)}) %all-to-all-start.5) | async-done | bytes 140704 | tf_op jit(solution)/shard_map/all_to_all | solution.py:704
  (222 shorter events, 80.5 us)
Async XLA Ops:
  7.2 95.7 %all-gather.2.cloned.1.call-start = ((), (), s32[]{:S(2)}) async-start(), calls=%async_computation.8 | async-start | bytes 4866048 | tf_op jit(solution)/shard_map/all_gather | solution.py:630
  8.5 10.9 %collective-permute-start = (bf16[24,1920]{1,0:T(8,128)(2,1)S(1)}, bf16[24,1920]{1,0:T(8,128)(2,1)S(1)}, u32[]{:S(2)}, u32[]{:S(2)}) collective-permute-start(bf16[24,1920]{1,0:T(8,128)(2,1)S(1)} %get-tuple-element.182), channel_id=1, source_target_pairs={{0,1},{1,0},{2,3},{3,2},{4,5},{5,4},{6,7},{7,6},{8,9},{9,8},{10,11... | collective-permute-start | bytes 276488 | tf_op jit(solution)/shard_map/ppermute | solution.py:50
  11.5 10.0 %collective-permute-start.1 = (bf16[24,1920]{1,0:T(8,128)(2,1)S(1)}, bf16[24,1920]{1,0:T(8,128)(2,1)S(1)}, u32[]{:S(2)}, u32[]{:S(2)}) collective-permute-start(bf16[24,1920]{1,0:T(8,128)(2,1)S(1)} %get-tuple-element.182), channel_id=1, source_target_pairs={{0,2},{1,3},{2,0},{3,1},{4,6},{5,7},{6,4},{7,5},{8,10},{9,11},{10,... | collective-permute-start | bytes 276488 | tf_op jit(solution)/shard_map/ppermute | solution.py:50
  14.1 7.4 %collective-permute-start.2 = (bf16[24,1920]{1,0:T(8,128)(2,1)S(1)}, bf16[24,1920]{1,0:T(8,128)(2,1)S(1)}, u32[]{:S(2)}, u32[]{:S(2)}) collective-permute-start(bf16[24,1920]{1,0:T(8,128)(2,1)S(1)} %get-tuple-element.182), channel_id=1, source_target_pairs={{0,3},{1,2},{2,1},{3,0},{4,7},{5,6},{6,5},{7,4},{8,11},{9,10},{10,... | collective-permute-start | bytes 276488 | tf_op jit(solution)/shard_map/ppermute | solution.py:50
  14.9 6.7 %collective-permute-start.3 = (bf16[16,768]{1,0:T(8,128)(2,1)S(1)}, bf16[16,768]{1,0:T(8,128)(2,1)S(1)}, u32[]{:S(2)}, u32[]{:S(2)}) collective-permute-start(bf16[16,768]{1,0:T(8,128)(2,1)S(1)} %slice.126), channel_id=1, source_target_pairs={{0,1},{1,2},{2,3},{3,4},{4,5},{5,6},{6,7},{7,8},{8,9},{9,10},{10,1... | collective-permute-start | bytes 73736 | tf_op jit(solution)/shard_map/ppermute | solution.py:46
  25.4 15.5 %collective-permute-start.4 = (bf16[96,1920]{1,0:T(8,128)(2,1)S(1)}, bf16[96,1920]{1,0:T(8,128)(2,1)}, u32[]{:S(2)}, u32[]{:S(2)}) collective-permute-start(bf16[96,1920]{1,0:T(8,128)(2,1)S(1)} %constant_dynamic-update-slice_fusion.others_0_), channel_id=1, source_target_pairs={{0,8},{4,12},{8,0},{12,4},{16,24},{20,28},{24,16},{28,20},{1,9},{5... | collective-permute-start | bytes 1105928 | tf_op jit(solution)/shard_map/ppermute | solution.py:50
  28.4 18.6 %collective-permute-start.5 = (bf16[96,1920]{1,0:T(8,128)(2,1)S(1)}, bf16[96,1920]{1,0:T(8,128)(2,1)}, u32[]{:S(2)}, u32[]{:S(2)}) collective-permute-start(bf16[96,1920]{1,0:T(8,128)(2,1)S(1)} %constant_dynamic-update-slice_fusion.others_0_), channel_id=1, source_target_pairs={{0,16},{4,20},{8,24},{12,28},{16,0},{20,4},{24,8},{28,12},{1,17},{... | collective-permute-start | bytes 1105928 | tf_op jit(solution)/shard_map/ppermute | solution.py:50
  29.9 17.1 %collective-permute-start.6 = (bf16[96,1920]{1,0:T(8,128)(2,1)S(1)}, bf16[96,1920]{1,0:T(8,128)(2,1)}, u32[]{:S(2)}, u32[]{:S(2)}) collective-permute-start(bf16[96,1920]{1,0:T(8,128)(2,1)S(1)} %constant_dynamic-update-slice_fusion.others_0_), channel_id=1, source_target_pairs={{0,24},{4,28},{8,16},{12,20},{16,8},{20,12},{24,0},{28,4},{1,25},{... | collective-permute-start | bytes 1105928 | tf_op jit(solution)/shard_map/ppermute | solution.py:50
  47.0 3.5 %collective-permute-start.10 = (bf16[96,1920]{1,0:T(8,128)(2,1)}, bf16[96,1920]{1,0:T(8,128)(2,1)}, u32[]{:S(2)}, u32[]{:S(2)}) collective-permute-start(bf16[96,1920]{1,0:T(8,128)(2,1)} %collective-permute-done.6.others_3_), channel_id=1, source_target_pairs={{0,4},{4,0},{8,12},{12,8},{16,20},{20,16},{24,28},{28,24},{1,5},{5... | collective-permute-start | bytes 1105928 | tf_op jit(solution)/shard_map/ppermute | solution.py:50
  47.0 3.5 %collective-permute-start.7 = (bf16[96,1920]{1,0:T(8,128)(2,1)S(1)}, bf16[96,1920]{1,0:T(8,128)(2,1)}, u32[]{:S(2)}, u32[]{:S(2)}) collective-permute-start(bf16[96,1920]{1,0:T(8,128)(2,1)S(1)} %constant_dynamic-update-slice_fusion.others_0_), channel_id=1, source_target_pairs={{0,4},{4,0},{8,12},{12,8},{16,20},{20,16},{24,28},{28,24},{1,5},{5... | collective-permute-start | bytes 1105928 | tf_op jit(solution)/shard_map/ppermute | solution.py:50
  47.5 3.0 collective-permute-start.8
  47.6 3.0 collective-permute-start.9
  75.0 19.7 %all-to-all-start = ((bf16[32,50,128]{2,1,0:T(8,128)(2,1)}), bf16[32,50,128]{2,1,0:T(8,128)(2,1)}, u32[]{:S(2)}, u32[]{:S(2)}) async-start(bf16[32,50,128]{2,1,0:T(8,128)(2,1)} %pad_maximum_fusion.5), calls=%async_computation | async-start | bytes 917504 | tf_op jit(solution)/shard_map/all_to_all | solution.py:704
  98.4 19.2 %all-to-all-start.1 = ((bf16[32,48,128]{2,1,0:T(8,128)(2,1)}), bf16[32,48,128]{2,1,0:T(8,128)(2,1)S(1)}, u32[]{:S(2)}, u32[]{:S(2)}) async-start(bf16[32,48,128]{2,1,0:T(8,128)(2,1)} %shard_map.206), calls=%async_computation.1 | async-start | bytes 786432 | tf_op jit(solution)/shard_map/all_to_all | solution.py:704
  142.5 23.2 %all-to-all-start.2 = ((bf16[32,48,128]{2,1,0:T(8,128)(2,1)}), bf16[32,48,128]{2,1,0:T(8,128)(2,1)S(1)}, u32[]{:S(2)}, u32[]{:S(2)}) async-start(bf16[32,48,128]{2,1,0:T(8,128)(2,1)} %bitcast.79), calls=%async_computation.2 | async-start | bytes 786432 | tf_op jit(solution)/shard_map/all_to_all | solution.py:704
  180.6 17.7 %all-to-all-start.3 = ((bf16[32,48,128]{2,1,0:T(8,128)(2,1)}), bf16[32,48,128]{2,1,0:T(8,128)(2,1)S(1)}, u32[]{:S(2)}, u32[]{:S(2)}) async-start(bf16[32,48,128]{2,1,0:T(8,128)(2,1)} %shard_map.209), calls=%async_computation.3 | async-start | bytes 786432 | tf_op jit(solution)/shard_map/all_to_all | solution.py:704
  186.4 68.0 %reduce-scatter.3.cloned.1.call-start = ((), (), s32[]{:S(2)}) async-start(), calls=%async_computation.9 | async-start | bytes 5308416 | tf_op jit(solution)/shard_map/reduce_scatter | solution.py:851
  233.8 7.9 %collective-permute-start.11 = (f32[8,1920]{1,0:T(8,128)}, f32[8,1920]{1,0:T(8,128)S(1)}, u32[]{:S(2)}, u32[]{:S(2)}) collective-permute-start(f32[8,1920]{1,0:T(8,128)} %get-tuple-element.121), channel_id=1, source_target_pairs={{1,0},{2,1},{3,2},{4,3},{5,4},{6,5},{7,6},{8,7},{9,8},{10,9},{11,1... | collective-permute-start | bytes 184328 | tf_op jit(solution)/shard_map/ppermute | solution.py:46
  247.2 4.7 %collective-permute-start.12 = (bf16[96,1920]{1,0:T(8,128)(2,1)S(1)}, bf16[96,1920]{1,0:T(8,128)(2,1)}, u32[]{:S(2)}, u32[]{:S(2)}) collective-permute-start(bf16[96,1920]{1,0:T(8,128)(2,1)S(1)} %get-tuple-element.163), channel_id=1, source_target_pairs={{0,4},{4,0},{8,12},{12,8},{16,20},{20,16},{24,28},{28,24},{1,5},{5... | collective-permute-start | bytes 1105928 | tf_op jit(solution)/shard_map/ppermute | solution.py:50
  250.0 2.0 collective-permute-start.13
  250.1 2.4 collective-permute-start.14
  251.8 23.2 %collective-permute-start.15 = (bf16[96,1920]{1,0:T(8,128)(2,1)S(1)}, bf16[96,1920]{1,0:T(8,128)(2,1)}, u32[]{:S(2)}, u32[]{:S(2)}) collective-permute-start(bf16[96,1920]{1,0:T(8,128)(2,1)S(1)} %get-tuple-element.160), channel_id=1, source_target_pairs={{0,4},{4,0},{8,12},{12,8},{16,20},{20,16},{24,28},{28,24},{1,5},{5... | collective-permute-start | bytes 1105928 | tf_op jit(solution)/shard_map/ppermute | solution.py:50
  254.4 20.7 %collective-permute-start.16 = (bf16[96,1920]{1,0:T(8,128)(2,1)S(1)}, bf16[96,1920]{1,0:T(8,128)(2,1)}, u32[]{:S(2)}, u32[]{:S(2)}) collective-permute-start(bf16[96,1920]{1,0:T(8,128)(2,1)S(1)} %get-tuple-element.134), channel_id=1, source_target_pairs={{0,8},{4,12},{8,0},{12,4},{16,24},{20,28},{24,16},{28,20},{1,9},{5... | collective-permute-start | bytes 1105928 | tf_op jit(solution)/shard_map/ppermute | solution.py:50
  255.9 19.1 %collective-permute-start.17 = (bf16[96,1920]{1,0:T(8,128)(2,1)S(1)}, bf16[96,1920]{1,0:T(8,128)(2,1)}, u32[]{:S(2)}, u32[]{:S(2)}) collective-permute-start(bf16[96,1920]{1,0:T(8,128)(2,1)S(1)} %get-tuple-element.135), channel_id=1, source_target_pairs={{0,16},{4,20},{8,24},{12,28},{16,0},{20,4},{24,8},{28,12},{1,17},{... | collective-permute-start | bytes 1105928 | tf_op jit(solution)/shard_map/ppermute | solution.py:50
  256.7 18.4 %collective-permute-start.18 = (bf16[96,1920]{1,0:T(8,128)(2,1)S(1)}, bf16[96,1920]{1,0:T(8,128)(2,1)}, u32[]{:S(2)}, u32[]{:S(2)}) collective-permute-start(bf16[96,1920]{1,0:T(8,128)(2,1)S(1)} %get-tuple-element.136), channel_id=1, source_target_pairs={{0,24},{4,28},{8,16},{12,20},{16,8},{20,12},{24,0},{28,4},{1,25},{... | collective-permute-start | bytes 1105928 | tf_op jit(solution)/shard_map/ppermute | solution.py:50
  258.6 16.4 %all-to-all-start.4 = ((f32[32,1,331]{2,1,0:T(1,128)}), f32[32,1,331]{2,1,0:T(1,128)S(1)}, u32[]{:S(2)}, u32[]{:S(2)}) async-start(f32[32,1,331]{2,1,0:T(1,128)} %all_to_all.30), calls=%async_computation.6 | async-start | bytes 98304 | tf_op jit(solution)/shard_map/all_to_all | solution.py:704
  261.2 37.3 %reduce-scatter.5.cloned.1.call-start = ((), (), s32[]{:S(2)}) async-start(), calls=%async_computation.10 | async-start | bytes 737280 | tf_op jit(solution)/shard_map/reduce_scatter | solution.py:955
  272.1 28.2 %copy-start.17 = (f32[48,768]{1,0:T(8,128)S(1)}, f32[48,768]{1,0:T(8,128)}, u32[]{:S(2)}) copy-start(f32[48,768]{1,0:T(8,128)} %param.16) | copy-start | bytes 442372
  276.9 10.0 %collective-permute-start.19 = (bf16[24,1920]{1,0:T(8,128)(2,1)S(1)}, bf16[24,1920]{1,0:T(8,128)(2,1)S(1)}, u32[]{:S(2)}, u32[]{:S(2)}) collective-permute-start(bf16[24,1920]{1,0:T(8,128)(2,1)S(1)} %get-tuple-element.169), channel_id=1, source_target_pairs={{0,1},{1,0},{2,3},{3,2},{4,5},{5,4},{6,7},{7,6},{8,9},{9,8},{10,11... | collective-permute-start | bytes 276488 | tf_op jit(solution)/shard_map/ppermute | solution.py:50
  277.7 12.2 %collective-permute-start.20 = (bf16[24,1920]{1,0:T(8,128)(2,1)S(1)}, bf16[24,1920]{1,0:T(8,128)(2,1)S(1)}, u32[]{:S(2)}, u32[]{:S(2)}) collective-permute-start(bf16[24,1920]{1,0:T(8,128)(2,1)S(1)} %get-tuple-element.171), channel_id=1, source_target_pairs={{0,2},{1,3},{2,0},{3,1},{4,6},{5,7},{6,4},{7,5},{8,10},{9,11},{10,... | collective-permute-start | bytes 276488 | tf_op jit(solution)/shard_map/ppermute | solution.py:50
  278.2 12.9 %collective-permute-start.21 = (bf16[24,1920]{1,0:T(8,128)(2,1)S(1)}, bf16[24,1920]{1,0:T(8,128)(2,1)S(1)}, u32[]{:S(2)}, u32[]{:S(2)}) collective-permute-start(bf16[24,1920]{1,0:T(8,128)(2,1)S(1)} %get-tuple-element.170), channel_id=1, source_target_pairs={{0,3},{1,2},{2,1},{3,0},{4,7},{5,6},{6,5},{7,4},{8,11},{9,10},{10,... | collective-permute-start | bytes 276488 | tf_op jit(solution)/shard_map/ppermute | solution.py:50
  282.1 14.5 %all-to-all-start.5 = ((f32[32,1,1099]{2,1,0:T(1,128)}), f32[32,1,1099]{2,1,0:T(1,128)S(1)}, u32[]{:S(2)}, u32[]{:S(2)}) async-start(f32[32,1,1099]{2,1,0:T(1,128)} %broadcast_in_dim.17), calls=%async_computation.7 | async-start | bytes 294912 | tf_op jit(solution)/shard_map/all_to_all | solution.py:704
  (37 other events, 339.2 us)
Sparse Core Ops, SparseCore 0:
  21.7 69.5 all-gather.1
  198.4 53.1 reduce-scatter.2
  264.4 26.1 reduce-scatter.4
